TPU v7x, 32 devices: a whole 2x2x4 slice. The times are simulated.
32 devices in a mesh: parts: 2 (over y), branch: 2 (over x), seq: 4 (over z), head: 2 (over core).
Axes of the slice: x: 2, y: 2, z: 4, core: 2. Of those that a mesh axis runs over, the one named last changes fastest.
Arguments:
- queries: bfloat16 [4, 48, 8, 128], P(('parts', 'branch'), 'seq', 'head'), parts along dimension 0, may hold values from -160 to 160
- output_cotangent: bfloat16 [4, 48, 8, 128], P(('parts', 'branch'), 'seq', 'head'), parts along dimension 0, may hold values from -6 to 6
- root_keys: bfloat16 [4096, 128], P(('parts', 'seq')), parts along dimension 0, may hold values from -8 to 8
- root_values: bfloat16 [4096, 128], P(('parts', 'seq')), parts along dimension 0, may hold values from -6 to 6
- branch_keys: bfloat16 [4, 2048, 128], P(('parts', 'branch'), 'seq'), parts along dimension 0, may hold values from -6 to 6
- branch_values: bfloat16 [4, 2048, 128], P(('parts', 'branch'), 'seq'), parts along dimension 0, may hold values from -6 to 6
- answer_positions: int32 [4, 48], P(('parts', 'branch')), parts along dimension 0, may hold values from 0 to 2047, as said below
Outputs:
- attention: bfloat16 [4, 48, 8, 128], P(('parts', 'branch'), 'seq', 'head'), parts along dimension 0
- query_gradient: float32 [4, 48, 8, 128], P(('parts', 'branch'), 'seq', 'head'), parts along dimension 0
- root_key_gradient: float32 [4096, 128], P(('parts', 'seq')), parts along dimension 0
- root_value_gradient: float32 [4096, 128], P(('parts', 'seq')), parts along dimension 0
- branch_key_gradient: float32 [4, 2048, 128], P(('parts', 'branch'), 'seq'), parts along dimension 0
- branch_value_gradient: float32 [4, 2048, 128], P(('parts', 'branch'), 'seq'), parts along dimension 0
There are 2 independent parts, one for each index of `parts`. A program takes and returns all parts, laid end to end along the dimension named above; each array names one. Nothing has to cross between parts.
Inputs may be any that keep to these rules, and one draw needn't show every extreme that they name: `answer_positions`: within each branch the positions are strictly increasing.
All inputs are finite; a program needn't handle non-finite values.
Results may differ from a plain program's by a relative error of at most 0.015.
Values may be sent and summed in bfloat16 or wider, within the bound.
A program may use at most 64 MiB of HBM per device.

v0:
```python
import math

import jax
import jax.numpy as jnp
from jax import lax
from jax.sharding import PartitionSpec as P

NEG = -1e30


def contract_rows(left, right):
    return lax.dot_general(
        left, right, (((0,), (0,)), ((), ())), preferred_element_type=jnp.float32
    )


def contract_last(left, right):
    return lax.dot_general(
        left, right, (((1,), (1,)), ((), ())), preferred_element_type=jnp.float32
    )


def per_device(
    queries, output_cotangent, root_keys, root_values, branch_keys, branch_values, answer_positions
):
    head_width = queries.shape[3]
    heads_here = queries.shape[2]
    score_scale = 1.0 / math.sqrt(head_width)
    root_count = root_keys.shape[0]
    branch_count = branch_keys.shape[1]
    seq_index = lax.axis_index("seq")
    gathered_query, gathered_grad = (
        lax.all_gather(queries, "seq", axis=1, tiled=True),
        lax.all_gather(output_cotangent, "seq", axis=1, tiled=True),
    )
    answers = gathered_query.shape[1]
    row_total = answers * heads_here
    query_rows = gathered_query[0].reshape(row_total, head_width)
    grad_rows = gathered_grad[0].reshape(row_total, head_width)
    row_places = jnp.repeat(answer_positions[0], heads_here)
    all_keys = jnp.concatenate([root_keys, branch_keys[0]], 0)
    all_values = jnp.concatenate([root_values, branch_values[0]], 0)
    local_index = jnp.arange(root_count + branch_count, dtype=jnp.int32)
    key_places = jnp.where(
        local_index < root_count, -1, seq_index * branch_count + local_index - root_count
    )
    block_rows = 512 if row_total % 512 == 0 else row_total
    block_count = row_total // block_rows
    query_blocks = query_rows.reshape(block_count, block_rows, head_width)
    grad_blocks = grad_rows.reshape(block_count, block_rows, head_width)
    place_blocks = row_places.reshape(block_count, block_rows)

    def masked_logits(query_block, place_block):
        logits = contract_last(query_block, all_keys) * score_scale
        return jnp.where(key_places[None, :] <= place_block[:, None], logits, NEG)

    def forward_block(pieces):
        logits = masked_logits(pieces[0], pieces[1])
        peak = jnp.max(logits, axis=1)
        probs = jnp.exp(logits - peak[:, None])
        weighted = jnp.dot(
            probs.astype(jnp.bfloat16), all_values, preferred_element_type=jnp.float32
        )
        return (weighted, jnp.sum(probs, axis=1), peak)

    weighted_local, totals_local, peaks_local = lax.map(forward_block, (query_blocks, place_blocks))
    weighted_local = weighted_local.reshape(answers, heads_here, head_width)
    totals_local = totals_local.reshape(answers, heads_here)
    peaks_local = peaks_local.reshape(answers, heads_here)
    peaks_each, weighted_each, totals_each = (
        lax.all_to_all(peaks_local[None], "seq", split_axis=1, concat_axis=0, tiled=True),
        lax.all_to_all(weighted_local[None], "seq", split_axis=1, concat_axis=0, tiled=True),
        lax.all_to_all(totals_local[None], "seq", split_axis=1, concat_axis=0, tiled=True),
    )
    peaks_own = jnp.max(peaks_each, axis=0)
    factor = jnp.exp(peaks_each - peaks_own[None])
    weighted_own = jnp.sum(weighted_each * factor[..., None], axis=0)
    totals_own = jnp.sum(totals_each * factor, axis=0)
    attended_exact = weighted_own / totals_own[..., None]
    attended = attended_exact.astype(jnp.bfloat16)
    lse_own = peaks_own + jnp.log(totals_own)
    delta_own = jnp.sum(output_cotangent[0].astype(jnp.float32) * attended_exact, axis=-1)
    lse_all, delta_all = (
        lax.all_gather(lse_own, "seq", axis=0, tiled=True),
        lax.all_gather(delta_own, "seq", axis=0, tiled=True),
    )
    lse_blocks = lse_all.reshape(block_count, block_rows)
    delta_blocks = delta_all.reshape(block_count, block_rows)

    def backward_block(running, pieces):
        query_block, grad_block, place_block, lse_block, delta_block = pieces
        logits = masked_logits(query_block, place_block)
        weights = jnp.exp(logits - lse_block[:, None])
        value_sum = running[1] + contract_rows(weights.astype(jnp.bfloat16), grad_block)
        product = contract_last(grad_block, all_values)
        slope = (weights * (product - delta_block[:, None])).astype(jnp.bfloat16)
        query_term = jnp.dot(slope, all_keys, preferred_element_type=jnp.float32) * score_scale
        key_sum = running[0] + contract_rows(slope, query_block) * score_scale
        return ((key_sum, value_sum), query_term)

    empty = jnp.zeros((root_count + branch_count, head_width), jnp.float32)
    sums, query_terms = lax.scan(
        backward_block,
        (empty, empty),
        (query_blocks, grad_blocks, place_blocks, lse_blocks, delta_blocks),
    )
    key_sum, value_sum = sums
    query_terms = query_terms.reshape(answers, heads_here, head_width)
    query_own = lax.psum_scatter(query_terms, "seq", scatter_dimension=0, tiled=True)
    root_key_sum, root_value_sum = lax.psum(
        (key_sum[:root_count], value_sum[:root_count]), ("branch", "head")
    )
    branch_key_sum, branch_value_sum = lax.psum(
        (key_sum[root_count:], value_sum[root_count:]), "head"
    )
    return (
        attended[None],
        query_own[None],
        root_key_sum,
        root_value_sum,
        branch_key_sum[None],
        branch_value_sum[None],
    )


def solution(mesh):
    placed = (
        P(("parts", "branch"), "seq", "head", None),
        P(("parts", "branch"), "seq", "head", None),
        P(("parts", "seq"), None),
        P(("parts", "seq"), None),
        P(("parts", "branch"), "seq", None),
        P(("parts", "branch"), "seq", None),
        P(("parts", "branch"), None),
    )
    return jax.shard_map(
        per_device,
        mesh=mesh,
        in_specs=placed,
        out_specs=(
            P(("parts", "branch"), "seq", "head", None),
            P(("parts", "branch"), "seq", "head", None),
            P(("parts", "seq"), None),
            P(("parts", "seq"), None),
            P(("parts", "branch"), "seq", None),
            P(("parts", "branch"), "seq", None),
        ),
        check_vma=False,
    )
```

profile of v0, /device:TPU:0, one launch (start us, length us, event | category | flops | bytes accessed | tf_op | source)
XLA Modules:
  0.0 189.0 jit_solution(4839453067284485619)
XLA Ops:
  7.2 0.0 copy-start.7
  7.2 0.6 copy-done.7
  7.8 0.1 broadcast_in_dim.53
  7.9 0.1 le.37
  8.0 0.6 copy-done.6
  8.6 14.7 %all_gather.12 = bf16[1,48,4,128]{3,2,0,1:T(4,128)(2,1)S(1)} all-gather(bf16[1,12,4,128]{3,2,0,1:T(4,128)(2,1)S(1)} %bitcast.60), channel_id=1, replica_groups=mesh['parts'=2,'branch'=2,'seq'=4,'head'=2] {'seq'}, dimensions={1}, use_global_device_ids=true | all-gather | bytes 61440 | tf_op jit(solution)/shard_map/all_gather | solution.py:33
  23.4 1.3 fusion.20
  24.7 0.0 copy-start
  24.7 0.0 copy-start.1
  24.7 0.3 fusion.5
  25.0 0.7 broadcast_in_dim_reshape.11
  25.7 4.8 %all-to-all-start.2 = ((f32[1,48,4]{2,0,1:T(1,128)}), f32[1,48,4]{2,0,1:T(1,128)S(1)}, u32[]{:S(2)}, u32[]{:S(2)}) async-start(f32[1,48,4]{2,0,1:T(1,128)} %bitcast.11), calls=%async_computation.2 | async-start | bytes 49152 | tf_op jit(solution)/shard_map/all_to_all | solution.py:73
  30.5 1.0 fusion.10
  31.5 0.7 broadcast_in_dim_reshape.10
  32.2 3.9 %all-to-all-done.2 = f32[1,48,4]{2,0,1:T(1,128)S(1)} async-done(((f32[1,48,4]{2,0,1:T(1,128)}), f32[1,48,4]{2,0,1:T(1,128)S(1)}, u32[]{:S(2)}, u32[]{:S(2)}) %all-to-all-start.2) | async-done | bytes 800 | tf_op jit(solution)/shard_map/all_to_all | solution.py:73
  36.1 3.4 %all-to-all-start.1 = ((f32[1,48,4]{2,0,1:T(1,128)}), f32[1,48,4]{2,0,1:T(1,128)S(1)}, u32[]{:S(2)}, u32[]{:S(2)}) async-start(f32[1,48,4]{2,0,1:T(1,128)} %bitcast.9), calls=%async_computation.1 | async-start | bytes 49152 | tf_op jit(solution)/shard_map/all_to_all | solution.py:71
  39.6 13.6 %all_gather.14 = bf16[1,48,4,128]{3,2,0,1:T(4,128)(2,1)S(1)} all-gather(bf16[1,12,4,128]{3,2,0,1:T(4,128)(2,1)S(1)} %bitcast.59), channel_id=1, replica_groups=mesh['parts'=2,'branch'=2,'seq'=4,'head'=2] {'seq'}, dimensions={1}, use_global_device_ids=true | all-gather | bytes 61440 | tf_op jit(solution)/shard_map/all_gather | solution.py:34
  53.2 0.1 copy.29
  53.3 0.1 all_to_all.32
  53.3 0.0 all-to-all-done.1
  53.3 4.5 %all-to-all-start = ((f32[1,48,4,128]{3,2,0,1:T(4,128)}), f32[1,48,4,128]{3,2,0,1:T(4,128)S(1)}, u32[]{:S(2)}, u32[]{:S(2)}) async-start(f32[1,48,4,128]{3,2,0,1:T(4,128)} %bitcast.7), calls=%async_computation | async-start | bytes 196608 | tf_op jit(solution)/shard_map/all_to_all | solution.py:72
  57.8 0.1 copy.26
  57.9 0.1 all_to_all.30
  58.1 0.1 copy.30
  58.2 12.4 %all-gather = f32[4,12,4]{1,2,0:T(4,128)S(1)} all-gather(f32[1,12,4]{1,2,0:T(4,128)S(1)} %add_bitcast_fusion), channel_id=1, replica_groups=mesh['parts'=2,'branch'=2,'seq'=4,'head'=2] {'seq'}, dimensions={0}, use_global_device_ids=true | all-gather | bytes 960 | tf_op jit(solution)/shard_map/all_gather | solution.py:84
  70.6 0.1 copy.31
  70.7 0.1 sub.66
  70.8 0.1 copy.27
  70.9 0.4 fusion.8
  71.4 0.8 slice_bitcast_fusion
  72.2 0.0 all-to-all-done
  72.2 0.1 multiply_reduce_fusion
  72.3 0.2 fusion.15
  72.5 0.1 copy.34
  72.6 11.9 %all-gather.1 = f32[4,12,4]{1,2,0:T(4,128)S(1)} all-gather(f32[1,12,4]{1,2,0:T(4,128)S(1)} %bitcast.61), channel_id=1, replica_groups=mesh['parts'=2,'branch'=2,'seq'=4,'head'=2] {'seq'}, dimensions={0}, use_global_device_ids=true | all-gather | bytes 960 | tf_op jit(solution)/shard_map/all_gather | solution.py:85
  84.5 0.1 copy.35
  84.6 0.1 sub.69
  84.7 0.0 copy-start.8
  84.7 0.0 copy-start.9
  84.7 0.3 fusion.4
  85.0 0.6 copy-done.8
  85.6 0.1 copy-done.9
  85.6 0.9 convolution_multiply_fusion.2
  86.5 0.4 convolution_multiply_fusion.1
  86.9 0.0 all-reduce.7.cloned.1.call-update
  86.9 0.0 all-reduce.9.cloned.1.call-start
  87.0 0.8 slice_bitcast_fusion.1
  87.8 0.0 all-reduce.9.cloned.1.call-update
  87.8 0.0 all-reduce.11.cloned.1.call-start
  87.9 0.7 all-reduce.11.cloned.1.call-update
  88.5 0.0 copy-start.10
  88.6 0.6 copy-done.10
  89.2 0.6 dynamic-slice
  90.4 0.7 fusion.14
  91.1 28.8 %all-reduce.7.cloned.1.call-done = f32[48,4,128]{2,1,0:T(4,128)} async-done(((f32[48,4,128]{2,1,0:T(4,128)}), f32[48,4,128]{2,1,0:T(4,128)}) %all-reduce.7.cloned.1.call-update) | async-done | bytes 98320
  119.9 1.3 dynamic-slice_bitcast_fusion
  121.2 34.7 %all-reduce.9.cloned.1.call-done = (f32[512,128]{1,0:T(8,128)}, f32[512,128]{1,0:T(8,128)}) async-done(((f32[512,128]{1,0:T(8,128)}, f32[512,128]{1,0:T(8,128)}), (f32[512,128]{1,0:T(8,128)}, f32[512,128]{1,0:T(8,128)})) %all-reduce.9.cloned.1.call-update) | async-done | bytes 524304 | tf_op jit(solution)/shard_map/psum | solution.py:110
  155.9 22.1 %all-reduce.11.cloned.1.call-done = (f32[1,512,128]{2,1,0:T(8,128)}, f32[1,512,128]{2,1,0:T(8,128)}) async-done(((f32[1,512,128]{2,1,0:T(8,128)}, f32[1,512,128]{2,1,0:T(8,128)}), (f32[1,512,128]{2,1,0:T(8,128)}, f32[1,512,128]{2,1,0:T(8,128)})) %all-reduce.11.cloned.1.call-update) | async-done | bytes 524304 | tf_op jit(solution)/shard_map/psum | solution.py:113
  178.0 1.7 copy.41
  179.7 0.7 copy.42
  180.4 0.3 copy-done.4
  180.8 0.7 copy.43
  181.5 0.3 copy-done.3
  181.8 0.7 copy.44
  (14 shorter events, 0.1 us)
Async XLA Ops:
  7.2 0.7 copy-start.7
  7.9 0.7 copy-start.6
  24.7 5.8 %copy-start = (bf16[1,512,128]{2,1,0:T(8,128)(2,1)S(1)}, bf16[1,512,128]{2,1,0:T(8,128)(2,1)}, u32[]{:S(2)}) copy-start(bf16[1,512,128]{2,1,0:T(8,128)(2,1)} %param.12) | copy-start | bytes 393220
  24.7 5.8 %copy-start.1 = (bf16[512,128]{1,0:T(8,128)(2,1)S(1)}, bf16[512,128]{1,0:T(8,128)(2,1)}, u32[]{:S(2)}) copy-start(bf16[512,128]{1,0:T(8,128)(2,1)} %param.10) | copy-start | bytes 393220
  25.7 10.4 %all-to-all-start.2 = ((f32[1,48,4]{2,0,1:T(1,128)}), f32[1,48,4]{2,0,1:T(1,128)S(1)}, u32[]{:S(2)}, u32[]{:S(2)}) async-start(f32[1,48,4]{2,0,1:T(1,128)} %bitcast.11), calls=%async_computation.2 | async-start | bytes 49152 | tf_op jit(solution)/shard_map/all_to_all | solution.py:73
  36.1 3.4 %copy-start.5 = (bf16[1,12,4,128]{3,2,1,0:T(4,128)(2,1)S(1)}, bf16[1,12,4,128]{3,2,1,0:T(4,128)(2,1)}, u32[]{:S(2)}) copy-start(bf16[1,12,4,128]{3,2,1,0:T(4,128)(2,1)} %param.8) | copy-start | bytes 36868
  36.1 17.2 %all-to-all-start.1 = ((f32[1,48,4]{2,0,1:T(1,128)}), f32[1,48,4]{2,0,1:T(1,128)S(1)}, u32[]{:S(2)}, u32[]{:S(2)}) async-start(f32[1,48,4]{2,0,1:T(1,128)} %bitcast.9), calls=%async_computation.1 | async-start | bytes 49152 | tf_op jit(solution)/shard_map/all_to_all | solution.py:71
  53.3 18.8 %all-to-all-start = ((f32[1,48,4,128]{3,2,0,1:T(4,128)}), f32[1,48,4,128]{3,2,0,1:T(4,128)S(1)}, u32[]{:S(2)}, u32[]{:S(2)}) async-start(f32[1,48,4,128]{3,2,0,1:T(4,128)} %bitcast.7), calls=%async_computation | async-start | bytes 196608 | tf_op jit(solution)/shard_map/all_to_all | solution.py:72
  57.8 62.0 %all-reduce.7.cloned.1.call-start = ((), (), s32[]{:S(2)}) async-start(), calls=%async_computation.3 | async-start | bytes 196608
  84.7 0.9 copy-start.8
  84.7 1.0 copy-start.9
  86.9 69.0 %all-reduce.9.cloned.1.call-start = ((), (), s32[]{:S(2)}) async-start(), calls=%async_computation.4 | async-start | bytes 1048576 | tf_op jit(solution)/shard_map/psum | solution.py:110
  87.8 90.2 %all-reduce.11.cloned.1.call-start = ((), (), s32[]{:S(2)}) async-start(), calls=%async_computation.5 | async-start | bytes 1048576 | tf_op jit(solution)/shard_map/psum | solution.py:113
  88.5 0.7 copy-start.10
  178.0 1.7 copy-start.2
  179.7 1.0 copy-start.4
  180.8 1.0 copy-start.3
Sparse Core Ops, SparseCore 0:
  87.0 32.8 all-reduce.6
  123.0 32.8 all-reduce.8
  159.0 18.9 all-reduce.10
where the time goes:
time: 190 us; the launch traced here: 189 us
  waiting for transfers between devices  90.2 us (47%)
  blocking collectives  52.6 us (28%)
  between operations  14.5 us (8%)
  local copies, waits for them, and re-layouts  13.3 us (7%)
  starting transfers between devices  12.8 us (7%)
  matrix products  4.23 us (2%)
    psum x1, waiting for transfers between devices, per_device(): lax.psum((key_sum[:root_count], value_sum[:root_count]), ('branch', 'head'))  34.7 us
    unnamed x4, waiting for transfers between devices  29.5 us
    psum x1, waiting for transfers between devices, per_device(): lax.psum((key_sum[root_count:], value_sum[root_count:]), 'head')  22.1 us
    all_gather x1, blocking collectives, per_device(): lax.all_gather(queries, 'seq', axis=1, tiled=True)  14.7 us
    all_gather x1, blocking collectives, per_device(): lax.all_gather(output_cotangent, 'seq', axis=1, tiled=True)  13.6 us
    all_gather x1, blocking collectives, per_device(): lax.all_gather(lse_own, 'seq', axis=0, tiled=True)  12.4 us
    all_gather x1, blocking collectives, per_device(): lax.all_gather(delta_own, 'seq', axis=0, tiled=True)  11.9 us
    unnamed x27, local copies, waits for them, and re-layouts  7.69 us
  transfers between devices with their start and end apart: 6, of which 4 were waited for; matrix products, arithmetic and copies ran while one was open for 4% of the time, Pallas kernels for 0%

commit v1 on v0

v1 whole, which is shorter than its diff:
```python
import functools
import math

import jax
import jax.numpy as jnp
from jax import lax
from jax.experimental import pallas as pl
from jax.experimental.pallas import tpu as pltpu
from jax.sharding import PartitionSpec as P

NEG = -1e30
ROWS = 256
F32 = jnp.float32
BF16 = jnp.bfloat16


def dot_last(left, right):
    return lax.dot_general(left, right, (((1,), (1,)), ((), ())), preferred_element_type=F32)


def dot_first(left, right):
    return lax.dot_general(left, right, (((0,), (0,)), ((), ())), preferred_element_type=F32)


def dot_plain(left, right):
    return jnp.dot(left, right, preferred_element_type=F32)


def remote(src, dst, send, recv, device):
    return pltpu.make_async_remote_copy(
        src_ref=src,
        dst_ref=dst,
        send_sem=send,
        recv_sem=recv,
        device_id=device,
        device_id_type=pl.DeviceIdType.MESH,
    )


def over(count, body):
    if count == 1:
        body(0)
    else:
        lax.fori_loop(0, count, lambda at, carry: (body(at), carry)[1], 0)


def kernel(
    sizes,
    q_ref, g_ref, pos_ref, rk_hbm, rv_hbm, bk_hbm, bv_hbm,
    att_out, dq_out, rk_out, rv_out, bk_out, bv_out,
    keys, values, rows_f32, qbuf, gbuf, stats, probs, product, weighted, place,
    att_send, att_recv, dq_acc, dq_send, dq_recv,
    root_part, root_recv, root_all, branch_all, slope_root, slope_branch, grads,
    load_sem, q_ss, q_rs, g_ss, g_rs, st_ss, st_rs, at_ss, at_rs, dq_ss, dq_rs,
    rs_ss, rs_rs, x_ss, x_rs, hd_ss, hd_rs, br_ss, br_rs,
):
    n, heads, branches = sizes
    me, my_head, my_branch = (
        lax.axis_index("seq"), lax.axis_index("head"), lax.axis_index("branch")
    )
    answers, per, width = q_ref.shape[1:]
    own = answers * per
    padded = qbuf.shape[0]
    chunks = padded // ROWS
    root_rows, branch_rows = rk_hbm.shape[0], bk_hbm.shape[1]
    piece = root_rows // heads
    scale = 1.0 / math.sqrt(width)

    def seq_to(d):
        return {"seq": lax.rem(me + d, n)}

    def seq_from(d):
        return lax.rem(me - d + n, n)

    def head_to(d):
        return {"head": lax.rem(my_head + d, heads)}

    def head_from(d):
        return lax.rem(my_head - d + heads, heads)

    def branch_to(d):
        return {"branch": lax.rem(my_branch + d, branches)}

    def branch_from(d):
        return lax.rem(my_branch - d + branches, branches)

    barrier = pltpu.get_barrier_semaphore()
    for to, count in ((seq_to, n), (head_to, heads), (branch_to, branches)):
        for d in range(1, count):
            pl.semaphore_signal(
                barrier, inc=1, device_id=to(d), device_id_type=pl.DeviceIdType.MESH
            )

    loads = [
        pltpu.make_async_copy(rk_hbm, keys.at[pl.ds(0, root_rows)], load_sem.at[0]),
        pltpu.make_async_copy(bk_hbm.at[0], keys.at[pl.ds(root_rows, branch_rows)], load_sem.at[1]),
        pltpu.make_async_copy(rv_hbm, values.at[pl.ds(0, root_rows)], load_sem.at[2]),
        pltpu.make_async_copy(bv_hbm.at[0], values.at[pl.ds(root_rows, branch_rows)], load_sem.at[3]),
    ]
    for load in loads:
        load.start()

    mine = pl.ds(pl.multiple_of(me * own, 16), own)
    for at, (source, target) in enumerate(((q_ref, qbuf), (g_ref, gbuf))):
        for i in range(answers):
            rows_f32[at, i * per:(i + 1) * per, :] = source[0, i].astype(F32)
        target[mine, :] = rows_f32[at].astype(BF16)
        if padded > n * own:
            target[n * own:, :] = jnp.zeros((padded - n * own, width), BF16)

    pl.semaphore_wait(barrier, (n - 1) + (heads - 1) + (branches - 1))

    sends = []

    def send(*pieces):
        copy = remote(*pieces)
        copy.start()
        sends.append(copy)

    for buf, ss, rs in ((qbuf, q_ss, q_rs), (gbuf, g_ss, g_rs)):
        for d in range(1, n):
            send(buf.at[mine], buf.at[mine], ss.at[d - 1], rs.at[d - 1], seq_to(d))

    def arrived_rows(buf, ss, rs):
        for d in range(1, n):
            rows = pl.ds(pl.multiple_of(seq_from(d) * own, 16), own)
            remote(buf.at[rows], buf.at[rows], ss.at[d - 1], rs.at[d - 1], seq_to(d)).wait_recv()

    total = pos_ref.shape[1]
    spot = jnp.broadcast_to(pos_ref[...], (8, total))
    high = (spot >> 7).astype(F32).astype(BF16)
    low = (spot & 127).astype(F32).astype(BF16)

    def expand(c):
        row = lax.broadcasted_iota(jnp.int32, (total, ROWS), 1) + c * ROWS
        answer = lax.broadcasted_iota(jnp.int32, (total, ROWS), 0)
        pick = (row >= answer * per) & (row < answer * per + per)
        pick = jnp.where(pick, 1.0, 0.0).astype(BF16)
        place[c] = dot_plain(high, pick) * 128.0 + dot_plain(low, pick)

    over(chunks, expand)

    for load in loads:
        load.wait()
    arrived_rows(qbuf, q_ss, q_rs)

    key_place = (
        lax.broadcasted_iota(jnp.int32, (branch_rows, ROWS), 0) + me * branch_rows
    ).astype(F32)

    def rows_of(c):
        return pl.ds(c * ROWS if isinstance(c, int) else pl.multiple_of(c * ROWS, ROWS), ROWS)

    def scores(c):
        q = qbuf[rows_of(c), :]
        on_root = dot_last(keys[:root_rows, :], q) * scale
        on_branch = dot_last(keys[root_rows:, :], q) * scale
        on_branch = jnp.where(key_place <= place[c, 0:1, :], on_branch, NEG)
        peak = jnp.maximum(
            jnp.max(on_root, axis=0, keepdims=True), jnp.max(on_branch, axis=0, keepdims=True)
        )
        p_root = jnp.exp(on_root - peak)
        p_branch = jnp.exp(on_branch - peak)
        probs[c, :root_rows, :] = p_root
        probs[c, root_rows:, :] = p_branch
        sums = jnp.sum(p_root, axis=0, keepdims=True) + jnp.sum(p_branch, axis=0, keepdims=True)
        share = dot_first(values[:root_rows, :], p_root.astype(BF16))
        share = share + dot_first(values[root_rows:, :], p_branch.astype(BF16))
        weighted[c] = share
        stats[me, c, 0:1, :] = peak
        stats[me, c, 1:2, :] = sums

    over(chunks, scores)
    arrived_rows(gbuf, g_ss, g_rs)

    def dots(c):
        turned = gbuf[rows_of(c), :].astype(F32).T
        stats[me, c, 2:3, :] = jnp.sum(weighted[c] * turned, axis=0, keepdims=True)
        stats[me, c, 3:8, :] = jnp.zeros((5, ROWS), F32)

    over(chunks, dots)
    for d in range(1, n):
        send(stats.at[me], stats.at[me], st_ss.at[d - 1], st_rs.at[d - 1], seq_to(d))

    def products(c):
        g = gbuf[rows_of(c), :]
        product[c, :root_rows, :] = dot_last(values[:root_rows, :], g)
        product[c, root_rows:, :] = dot_last(values[root_rows:, :], g)

    over(chunks, products)
    for d in range(1, n):
        at = seq_from(d)
        remote(stats.at[at], stats.at[at], st_ss.at[d - 1], st_rs.at[d - 1], seq_to(d)).wait_recv()

    def combine(c):
        peak = stats[0, c, 0:1, :]
        for s in range(1, n):
            peak = jnp.maximum(peak, stats[s, c, 0:1, :])
        sums, dotted = jnp.zeros((1, ROWS), F32), jnp.zeros((1, ROWS), F32)
        for s in range(n):
            factor = jnp.exp(stats[s, c, 0:1, :] - peak)
            sums = sums + stats[s, c, 1:2, :] * factor
            dotted = dotted + stats[s, c, 2:3, :] * factor
        factor = jnp.exp(stats[me, c, 0:1, :] - peak) / sums
        place[c, 1:2, :] = factor
        place[c, 2:3, :] = dotted / sums

    over(chunks, combine)

    def backward(c, start, count, slope):
        rows = rows_of(c)
        weights = probs[c, start:start + count, :] * place[c, 1:2, :]
        value_term = dot_plain(weights.astype(BF16), gbuf[rows, :])
        gap = product[c, start:start + count, :] - place[c, 2:3, :]
        sloped = (weights * gap).astype(BF16)
        slope[c] = sloped
        key_term = dot_plain(sloped, qbuf[rows, :]) * scale
        return value_term, key_term

    def sweep(start, count, slope):
        if chunks == 1:
            return backward(0, start, count, slope)
        grads[0, :count, :] = jnp.zeros((count, width), F32)
        grads[1, :count, :] = jnp.zeros((count, width), F32)

        def add(c):
            value_term, key_term = backward(c, start, count, slope)
            grads[0, :count, :] += value_term
            grads[1, :count, :] += key_term

        over(chunks, add)
        return grads[0, :count, :], grads[1, :count, :]

    for at, term in enumerate(sweep(0, root_rows, slope_root)):
        root_part[at] = term.astype(BF16)
        for d in range(1, heads):
            far = pl.ds(pl.multiple_of(lax.rem(my_head + d, heads) * piece, 16), piece)
            send(
                root_part.at[at, far], root_recv.at[at, d - 1],
                rs_ss.at[at, d - 1], rs_rs.at[at, d - 1], head_to(d),
            )

    near = pl.ds(pl.multiple_of(my_head * piece, 16), piece)
    for at in range(2):
        term = root_part[at, near, :].astype(F32)
        for d in range(1, heads):
            remote(
                root_recv.at[at, d - 1], root_recv.at[at, d - 1],
                rs_ss.at[at, d - 1], rs_rs.at[at, d - 1], head_to(d),
            ).wait_recv()
            term = term + root_recv[at, d - 1].astype(F32)
        root_all[at, my_branch, my_head] = term.astype(BF16)
        block = root_all.at[at, my_branch, my_head]
        for d in range(1, branches):
            send(block, block, x_ss.at[at, d - 1], x_rs.at[at, d - 1], branch_to(d))
        for d in range(1, heads):
            send(block, block, hd_ss.at[at, 0, d - 1], hd_rs.at[at, 0, d - 1], head_to(d))

    for at, term in enumerate(sweep(root_rows, branch_rows, slope_branch)):
        branch_all[at, my_head] = term.astype(BF16)
        block = branch_all.at[at, my_head]
        for d in range(1, heads):
            send(block, block, br_ss.at[at, d - 1], br_rs.at[at, d - 1], head_to(d))

    def query_terms(c):
        term = dot_first(slope_root[c], keys[:root_rows, :])
        term = term + dot_first(slope_branch[c], keys[root_rows:, :])
        dq_send[rows_of(c), :] = (term * scale).astype(BF16)
        att_send[rows_of(c), :] = (weighted[c] * place[c, 1:2, :]).T.astype(BF16)

    over(chunks, query_terms)
    for buf, into, ss, rs in ((dq_send, dq_recv, dq_ss, dq_rs), (att_send, att_recv, at_ss, at_rs)):
        for d in range(1, n):
            far = pl.ds(pl.multiple_of(lax.rem(me + d, n) * own, 16), own)
            send(buf.at[far], into.at[d - 1], ss.at[d - 1], rs.at[d - 1], seq_to(d))

    for at in range(2):
        for d in range(1, branches):
            block = root_all.at[at, branch_from(d), my_head]
            remote(block, block, x_ss.at[at, d - 1], x_rs.at[at, d - 1], branch_to(d)).wait_recv()
            for e in range(1, heads):
                send(block, block, hd_ss.at[at, d, e - 1], hd_rs.at[at, d, e - 1], head_to(e))

    for at, out in ((0, bv_out), (1, bk_out)):
        for d in range(1, heads):
            block = branch_all.at[at, head_from(d)]
            remote(block, block, br_ss.at[at, d - 1], br_rs.at[at, d - 1], head_to(d)).wait_recv()
        term = branch_all[at, 0].astype(F32)
        for h in range(1, heads):
            term = term + branch_all[at, h].astype(F32)
        out[0] = term

    for at, (buf, into, ss, rs, out) in enumerate((
        (dq_send, dq_recv, dq_ss, dq_rs, dq_out), (att_send, att_recv, at_ss, at_rs, att_out)
    )):
        term = buf[mine, :].astype(F32)
        for d in range(1, n):
            remote(
                into.at[d - 1], into.at[d - 1], ss.at[d - 1], rs.at[d - 1], seq_to(d)
            ).wait_recv()
            term = term + into[d - 1].astype(F32)
        rows_f32[at] = term
        for i in range(answers):
            out[0, i] = rows_f32[at, i * per:(i + 1) * per, :].astype(out.dtype)

    for at, out in ((0, rv_out), (1, rk_out)):
        for b in range(branches):
            for d in range(1, heads):
                block = root_all.at[at, lax.rem(my_branch - b + branches, branches), head_from(d)]
                remote(
                    block, block, hd_ss.at[at, b, d - 1], hd_rs.at[at, b, d - 1], head_to(d)
                ).wait_recv()
        for h in range(heads):
            term = root_all[at, 0, h].astype(F32)
            for b in range(1, branches):
                term = term + root_all[at, b, h].astype(F32)
            out[h * piece:(h + 1) * piece, :] = term

    for copy in sends:
        copy.wait_send()


def per_device(sizes, queries, output_cotangent, root_keys, root_values, branch_keys,
               branch_values, answer_positions):
    n, heads, branches = sizes
    answers, per, width = queries.shape[1:]
    own = answers * per
    padded = -(-n * own // ROWS) * ROWS
    chunks = padded // ROWS
    root_rows, branch_rows = root_keys.shape[0], branch_keys.shape[1]
    key_rows = root_rows + branch_rows
    piece = root_rows // heads
    vmem = pl.BlockSpec(memory_space=pltpu.VMEM)
    whole = pl.BlockSpec(memory_space=pl.ANY)

    def sem(*shape):
        return pltpu.SemaphoreType.DMA(tuple(max(1, size) for size in shape))

    z, h, b = max(1, n - 1), max(1, heads - 1), max(1, branches - 1)
    scratch = [
        pltpu.VMEM((key_rows, width), BF16),
        pltpu.VMEM((key_rows, width), BF16),
        pltpu.VMEM((2, own, width), F32),
        pltpu.VMEM((padded, width), BF16),
        pltpu.VMEM((padded, width), BF16),
        pltpu.VMEM((n, chunks, 8, ROWS), F32),
        pltpu.VMEM((chunks, key_rows, ROWS), F32),
        pltpu.VMEM((chunks, key_rows, ROWS), F32),
        pltpu.VMEM((chunks, width, ROWS), F32),
        pltpu.VMEM((chunks, 8, ROWS), F32),
        pltpu.VMEM((padded, width), BF16),
        pltpu.VMEM((z, own, width), BF16),
        pltpu.VMEM((8, 128), F32),
        pltpu.VMEM((padded, width), BF16),
        pltpu.VMEM((z, own, width), BF16),
        pltpu.VMEM((2, root_rows, width), BF16),
        pltpu.VMEM((2, h, piece, width), BF16),
        pltpu.VMEM((2, branches, heads, piece, width), BF16),
        pltpu.VMEM((2, heads, branch_rows, width), BF16),
        pltpu.VMEM((chunks, root_rows, ROWS), BF16),
        pltpu.VMEM((chunks, branch_rows, ROWS), BF16),
        pltpu.VMEM((2, max(root_rows, branch_rows), width), F32),
        sem(4),
        sem(z), sem(z), sem(z), sem(z), sem(z), sem(z), sem(z), sem(z), sem(z), sem(z),
        sem(2, h), sem(2, h), sem(2, b), sem(2, b),
        sem(2, branches, h), sem(2, branches, h), sem(2, h), sem(2, h),
    ]
    outs = (
        jax.ShapeDtypeStruct(queries.shape, BF16),
        jax.ShapeDtypeStruct(queries.shape, F32),
        jax.ShapeDtypeStruct(root_keys.shape, F32),
        jax.ShapeDtypeStruct(root_values.shape, F32),
        jax.ShapeDtypeStruct(branch_keys.shape, F32),
        jax.ShapeDtypeStruct(branch_values.shape, F32),
    )
    return pl.pallas_call(
        functools.partial(kernel, sizes),
        out_shape=outs,
        in_specs=[vmem, vmem, vmem, whole, whole, whole, whole],
        out_specs=[vmem] * 6,
        scratch_shapes=scratch,
        compiler_params=pltpu.CompilerParams(
            collective_id=0, has_side_effects=True, vmem_limit_bytes=48 * 1024 * 1024
        ),
    )(queries, output_cotangent, answer_positions, root_keys, root_values, branch_keys, branch_values)


def solution(mesh):
    sizes = (mesh.shape["seq"], mesh.shape["head"], mesh.shape["branch"])
    rows = P(("parts", "branch"), "seq", "head", None)
    root = P(("parts", "seq"), None)
    branch = P(("parts", "branch"), "seq", None)
    return jax.shard_map(
        functools.partial(per_device, sizes),
        mesh=mesh,
        in_specs=(rows, rows, root, root, branch, branch, P(("parts", "branch"), None)),
        out_specs=(rows, rows, root, root, branch, branch),
        check_vma=False,
    )
```

time: 190 us -> 31.3 us (0.16)
  waiting for transfers between devices: 90.2 us -> 0 us
  blocking collectives: 52.6 us -> 0 us
  Pallas kernels: 0 us -> 20.6 us
  between operations: 14.5 us -> 0.66 us
  starting transfers between devices: 12.8 us -> 0 us
  matrix products: 4.23 us -> 0 us
  local copies, waits for them, and re-layouts: 13.3 us -> 9.69 us
    psum x2 -> x0, waiting for transfers between devices: 56.8 us -> none  [the longest x1 34.7 us: per_device(): lax.psum((key_sum[:root_count], value_sum[:root_count]), ('branch', 'head'))]
    all_gather x4 -> x0, blocking collectives: 52.6 us -> none  [the longest x1 14.7 us: per_device(): lax.all_gather(queries, 'seq', axis=1, tiled=True)]
    unnamed x4 -> x0, waiting for transfers between devices: 29.5 us -> none
    pallas_call x0 -> x1, Pallas kernels: none -> 20.6 us  [per_device(): pl.pallas_call(functools.partial(kernel, sizes), out_shape=outs, in_specs...]
    all_to_all x3 -> x0, starting transfers between devices: 12.7 us -> none  [the longest x1 4.8 us: per_device(): lax.all_to_all(totals_local[None], 'seq', split_axis=1, concat_axis=0, ti...]
    dot_general x6 -> x0, matrix products: 4.23 us -> none  [the longest x2 1.6 us: contract_last(): lax.dot_general(left, right, (((1,), (1,)), ((), ())), preferred_element_...]
    all_to_all x3 -> x0, waiting for transfers between devices: 3.95 us -> none  [the longest x1 3.95 us: per_device(): lax.all_to_all(totals_local[None], 'seq', split_axis=1, concat_axis=0, ti...]
    broadcast_in_dim x4 -> x0, local copies, waits for them, and re-layouts: 3.06 us -> none  [the longest x1 1.35 us: per_device(): query_own[None]]
  transfers between devices with their start and end apart: 6 -> 0, of which waited for: 4 -> 0; matrix products, arithmetic and copies ran while one was open for 4% -> 0% of each run, Pallas kernels for 0% -> 0%
where the time goes in v1:
time: 31.3 us; the launch traced here: 31 us
  Pallas kernels  20.6 us (66%)
  local copies, waits for them, and re-layouts  9.69 us (31%)
  between operations  0.66 us (2%)
    pallas_call x1, Pallas kernels, per_device(): pl.pallas_call(functools.partial(kernel, sizes), out_shape=outs, in_specs...  20.6 us
    unnamed x20, local copies, waits for them, and re-layouts  9.69 us

profile of v1, /device:TPU:0, one launch (start us, length us, event | category | flops | bytes accessed | tf_op | source)
XLA Modules:
  0.0 31.0 jit_solution(7524075200255556039)
XLA Ops:
  0.6 0.0 copy-start
  0.6 0.9 %copy-done = bf16[512,128]{1,0:T(8,128)(2,1)S(1)} copy-done((bf16[512,128]{1,0:T(8,128)(2,1)S(1)}, bf16[512,128]{1,0:T(8,128)(2,1)}, u32[]{:S(2)}) %copy-start) | copy-done | bytes 131096
  1.5 0.0 copy-start.1
  1.5 0.9 %copy-done.1 = bf16[512,128]{1,0:T(8,128)(2,1)S(1)} copy-done((bf16[512,128]{1,0:T(8,128)(2,1)S(1)}, bf16[512,128]{1,0:T(8,128)(2,1)}, u32[]{:S(2)}) %copy-start.1) | copy-done | bytes 131096
  2.4 0.0 copy-start.2
  2.4 0.9 %copy-done.2 = bf16[1,512,128]{2,1,0:T(8,128)(2,1)S(1)} copy-done((bf16[1,512,128]{2,1,0:T(8,128)(2,1)S(1)}, bf16[1,512,128]{2,1,0:T(8,128)(2,1)}, u32[]{:S(2)}) %copy-start.2) | copy-done | bytes 131096
  3.3 0.0 copy-start.3
  3.4 0.9 %copy-done.3 = bf16[1,512,128]{2,1,0:T(8,128)(2,1)S(1)} copy-done((bf16[1,512,128]{2,1,0:T(8,128)(2,1)S(1)}, bf16[1,512,128]{2,1,0:T(8,128)(2,1)}, u32[]{:S(2)}) %copy-start.3) | copy-done | bytes 131096
  4.3 0.0 copy-start.4
  4.3 0.7 %copy-done.4 = bf16[1,12,4,128]{3,2,1,0:T(4,128)(2,1)S(1)} copy-done((bf16[1,12,4,128]{3,2,1,0:T(4,128)(2,1)S(1)}, bf16[1,12,4,128]{3,2,1,0:T(4,128)(2,1)}, u32[]{:S(2)}) %copy-start.4) | copy-done | bytes 12312
  5.0 0.0 copy-start.5
  5.0 0.7 %copy-done.5 = bf16[1,12,4,128]{3,2,1,0:T(4,128)(2,1)S(1)} copy-done((bf16[1,12,4,128]{3,2,1,0:T(4,128)(2,1)S(1)}, bf16[1,12,4,128]{3,2,1,0:T(4,128)(2,1)}, u32[]{:S(2)}) %copy-start.5) | copy-done | bytes 12312
  5.7 0.0 copy-start.6
  5.7 0.7 %copy-done.6 = s32[1,48]{1,0:T(1,128)S(1)} copy-done((s32[1,48]{1,0:T(1,128)S(1)}, s32[1,48]{1,0:T(1,128)}, u32[]{:S(2)}) %copy-start.6) | copy-done | bytes 216
  6.3 20.6 %shard_map.118 = (bf16[1,12,4,128]{3,2,1,0:T(4,128)(2,1)S(1)}, f32[1,12,4,128]{3,2,1,0:T(4,128)S(1)}, f32[512,128]{1,0:T(8,128)S(1)}, f32[512,128]{1,0:T(8,128)S...) custom-call(bf16[1,12,4,128]{3,2,1,0:T(4,128)(2,1)S(1)} %copy-done.4, bf16[1,12,4,128]{3,2,1,0:T(4,128)(2,1)S(1)} %copy-done.5, ...), custom_call_target="tpu_custom_call" | custom-call | tf_op jit(solution)/shard_map/pallas_call | solution.py:376
  26.9 0.6 %copy.19 = bf16[1,12,4,128]{3,2,1,0:T(4,128)(2,1)} copy(bf16[1,12,4,128]{3,2,1,0:T(4,128)(2,1)S(1)} %get-tuple-element.12) | data formatting | bytes 24576
  27.5 0.6 %copy.20 = f32[1,12,4,128]{3,2,1,0:T(4,128)} copy(f32[1,12,4,128]{3,2,1,0:T(4,128)S(1)} %get-tuple-element.13) | data formatting | bytes 49152
  28.1 0.7 %copy.21 = f32[512,128]{1,0:T(8,128)} copy(f32[512,128]{1,0:T(8,128)S(1)} %get-tuple-element.14) | data formatting | bytes 524288
  28.8 0.7 %copy.22 = f32[512,128]{1,0:T(8,128)} copy(f32[512,128]{1,0:T(8,128)S(1)} %get-tuple-element.15) | data formatting | bytes 524288
  29.6 0.7 %copy.23 = f32[1,512,128]{2,1,0:T(8,128)} copy(f32[1,512,128]{2,1,0:T(8,128)S(1)} %get-tuple-element.16) | data formatting | bytes 524288
  30.3 0.7 %copy.24 = f32[1,512,128]{2,1,0:T(8,128)} copy(f32[1,512,128]{2,1,0:T(8,128)S(1)} %get-tuple-element.17) | data formatting | bytes 524288
Async XLA Ops:
  0.6 0.9 %copy-start = (bf16[512,128]{1,0:T(8,128)(2,1)S(1)}, bf16[512,128]{1,0:T(8,128)(2,1)}, u32[]{:S(2)}) copy-start(bf16[512,128]{1,0:T(8,128)(2,1)} %rk_hbm.1) | copy-start | bytes 393220
  1.5 0.9 %copy-start.1 = (bf16[512,128]{1,0:T(8,128)(2,1)S(1)}, bf16[512,128]{1,0:T(8,128)(2,1)}, u32[]{:S(2)}) copy-start(bf16[512,128]{1,0:T(8,128)(2,1)} %rv_hbm.1) | copy-start | bytes 393220
  2.4 0.9 %copy-start.2 = (bf16[1,512,128]{2,1,0:T(8,128)(2,1)S(1)}, bf16[1,512,128]{2,1,0:T(8,128)(2,1)}, u32[]{:S(2)}) copy-start(bf16[1,512,128]{2,1,0:T(8,128)(2,1)} %bk_hbm.1) | copy-start | bytes 393220
  3.3 0.9 %copy-start.3 = (bf16[1,512,128]{2,1,0:T(8,128)(2,1)S(1)}, bf16[1,512,128]{2,1,0:T(8,128)(2,1)}, u32[]{:S(2)}) copy-start(bf16[1,512,128]{2,1,0:T(8,128)(2,1)} %bv_hbm.1) | copy-start | bytes 393220
  4.3 0.7 %copy-start.4 = (bf16[1,12,4,128]{3,2,1,0:T(4,128)(2,1)S(1)}, bf16[1,12,4,128]{3,2,1,0:T(4,128)(2,1)}, u32[]{:S(2)}) copy-start(bf16[1,12,4,128]{3,2,1,0:T(4,128)(2,1)} %q_ref.1) | copy-start | bytes 36868
  5.0 0.7 %copy-start.5 = (bf16[1,12,4,128]{3,2,1,0:T(4,128)(2,1)S(1)}, bf16[1,12,4,128]{3,2,1,0:T(4,128)(2,1)}, u32[]{:S(2)}) copy-start(bf16[1,12,4,128]{3,2,1,0:T(4,128)(2,1)} %g_ref.1) | copy-start | bytes 36868
  5.7 0.7 %copy-start.6 = (s32[1,48]{1,0:T(1,128)S(1)}, s32[1,48]{1,0:T(1,128)}, u32[]{:S(2)}) copy-start(s32[1,48]{1,0:T(1,128)} %pos_ref.1) | copy-start | bytes 580

commit v2 on v1

--- a/solution.py
+++ b/solution.py
@@ -46,9 +46,9 @@
 
 def kernel(
     sizes,
-    q_ref, g_ref, pos_ref, rk_hbm, rv_hbm, bk_hbm, bv_hbm,
+    q_hbm, g_hbm, pos_hbm, rk_hbm, rv_hbm, bk_hbm, bv_hbm,
     att_out, dq_out, rk_out, rv_out, bk_out, bv_out,
-    keys, values, rows_f32, qbuf, gbuf, stats, probs, product, weighted, place,
+    rows_in, pos_ref, keys, values, rows_f32, qbuf, gbuf, stats, probs, product, weighted, place,
     att_send, att_recv, dq_acc, dq_send, dq_recv,
     root_part, root_recv, root_all, branch_all, slope_root, slope_branch, grads,
     load_sem, q_ss, q_rs, g_ss, g_rs, st_ss, st_rs, at_ss, at_rs, dq_ss, dq_rs,
@@ -58,7 +58,7 @@
     me, my_head, my_branch = (
         lax.axis_index("seq"), lax.axis_index("head"), lax.axis_index("branch")
     )
-    answers, per, width = q_ref.shape[1:]
+    answers, per, width = q_hbm.shape[1:]
     own = answers * per
     padded = qbuf.shape[0]
     chunks = padded // ROWS
@@ -92,6 +92,9 @@
             )
 
     loads = [
+        pltpu.make_async_copy(q_hbm.at[0], rows_in.at[0], load_sem.at[4]),
+        pltpu.make_async_copy(g_hbm.at[0], rows_in.at[1], load_sem.at[5]),
+        pltpu.make_async_copy(pos_hbm, pos_ref, load_sem.at[6]),
         pltpu.make_async_copy(rk_hbm, keys.at[pl.ds(0, root_rows)], load_sem.at[0]),
         pltpu.make_async_copy(bk_hbm.at[0], keys.at[pl.ds(root_rows, branch_rows)], load_sem.at[1]),
         pltpu.make_async_copy(rv_hbm, values.at[pl.ds(0, root_rows)], load_sem.at[2]),
@@ -101,9 +104,10 @@
         load.start()
 
     mine = pl.ds(pl.multiple_of(me * own, 16), own)
-    for at, (source, target) in enumerate(((q_ref, qbuf), (g_ref, gbuf))):
+    for at, target in enumerate((qbuf, gbuf)):
+        loads[at].wait()
         for i in range(answers):
-            rows_f32[at, i * per:(i + 1) * per, :] = source[0, i].astype(F32)
+            rows_f32[at, i * per:(i + 1) * per, :] = rows_in[at, i].astype(F32)
         target[mine, :] = rows_f32[at].astype(BF16)
         if padded > n * own:
             target[n * own:, :] = jnp.zeros((padded - n * own, width), BF16)
@@ -126,6 +130,7 @@
             rows = pl.ds(pl.multiple_of(seq_from(d) * own, 16), own)
             remote(buf.at[rows], buf.at[rows], ss.at[d - 1], rs.at[d - 1], seq_to(d)).wait_recv()
 
+    loads[2].wait()
     total = pos_ref.shape[1]
     spot = jnp.broadcast_to(pos_ref[...], (8, total))
     high = (spot >> 7).astype(F32).astype(BF16)
@@ -140,7 +145,7 @@
 
     over(chunks, expand)
 
-    for load in loads:
+    for load in loads[3:]:
         load.wait()
     arrived_rows(qbuf, q_ss, q_rs)
 
@@ -207,32 +212,30 @@
 
     over(chunks, combine)
 
-    def backward(c, start, count, slope):
-        rows = rows_of(c)
+    def value_term(c, start, count, slope):
         weights = probs[c, start:start + count, :] * place[c, 1:2, :]
-        value_term = dot_plain(weights.astype(BF16), gbuf[rows, :])
+        return dot_plain(weights.astype(BF16), gbuf[rows_of(c), :])
+
+    def key_term(c, start, count, slope):
+        weights = probs[c, start:start + count, :] * place[c, 1:2, :]
         gap = product[c, start:start + count, :] - place[c, 2:3, :]
         sloped = (weights * gap).astype(BF16)
         slope[c] = sloped
-        key_term = dot_plain(sloped, qbuf[rows, :]) * scale
-        return value_term, key_term
-
-    def sweep(start, count, slope):
+        return dot_plain(sloped, qbuf[rows_of(c), :]) * scale
+
+    def sweep(term, start, count, slope):
         if chunks == 1:
-            return backward(0, start, count, slope)
-        grads[0, :count, :] = jnp.zeros((count, width), F32)
-        grads[1, :count, :] = jnp.zeros((count, width), F32)
+            return term(0, start, count, slope)
+        grads[:count, :] = jnp.zeros((count, width), F32)
 
         def add(c):
-            value_term, key_term = backward(c, start, count, slope)
-            grads[0, :count, :] += value_term
-            grads[1, :count, :] += key_term
+            grads[:count, :] += term(c, start, count, slope)
 
         over(chunks, add)
-        return grads[0, :count, :], grads[1, :count, :]
-
-    for at, term in enumerate(sweep(0, root_rows, slope_root)):
-        root_part[at] = term.astype(BF16)
+        return grads[:count, :]
+
+    for at, term in enumerate((value_term, key_term)):
+        root_part[at] = sweep(term, 0, root_rows, slope_root).astype(BF16)
         for d in range(1, heads):
             far = pl.ds(pl.multiple_of(lax.rem(my_head + d, heads) * piece, 16), piece)
             send(
@@ -256,8 +259,8 @@
         for d in range(1, heads):
             send(block, block, hd_ss.at[at, 0, d - 1], hd_rs.at[at, 0, d - 1], head_to(d))
 
-    for at, term in enumerate(sweep(root_rows, branch_rows, slope_branch)):
-        branch_all[at, my_head] = term.astype(BF16)
+    for at, term in enumerate((value_term, key_term)):
+        branch_all[at, my_head] = sweep(term, root_rows, branch_rows, slope_branch).astype(BF16)
         block = branch_all.at[at, my_head]
         for d in range(1, heads):
             send(block, block, br_ss.at[at, d - 1], br_rs.at[at, d - 1], head_to(d))
@@ -320,6 +323,15 @@
         copy.wait_send()
 
 
+def hand_out(*refs):
+    sems = refs[12]
+    copies = [pltpu.make_async_copy(refs[i], refs[6 + i], sems.at[i]) for i in range(6)]
+    for copy in copies:
+        copy.start()
+    for copy in copies:
+        copy.wait()
+
+
 def per_device(sizes, queries, output_cotangent, root_keys, root_values, branch_keys,
                branch_values, answer_positions):
     n, heads, branches = sizes
@@ -331,13 +343,15 @@
     key_rows = root_rows + branch_rows
     piece = root_rows // heads
     vmem = pl.BlockSpec(memory_space=pltpu.VMEM)
-    whole = pl.BlockSpec(memory_space=pl.ANY)
+    whole = pl.BlockSpec(memory_space=pltpu.HBM)
 
     def sem(*shape):
         return pltpu.SemaphoreType.DMA(tuple(max(1, size) for size in shape))
 
     z, h, b = max(1, n - 1), max(1, heads - 1), max(1, branches - 1)
     scratch = [
+        pltpu.VMEM((2, answers, per, width), BF16),
+        pltpu.VMEM(answer_positions.shape, jnp.int32),
         pltpu.VMEM((key_rows, width), BF16),
         pltpu.VMEM((key_rows, width), BF16),
         pltpu.VMEM((2, own, width), F32),
@@ -359,8 +373,8 @@
         pltpu.VMEM((2, heads, branch_rows, width), BF16),
         pltpu.VMEM((chunks, root_rows, ROWS), BF16),
         pltpu.VMEM((chunks, branch_rows, ROWS), BF16),
-        pltpu.VMEM((2, max(root_rows, branch_rows), width), F32),
-        sem(4),
+        pltpu.VMEM((max(root_rows, branch_rows), width), F32),
+        sem(7),
         sem(z), sem(z), sem(z), sem(z), sem(z), sem(z), sem(z), sem(z), sem(z), sem(z),
         sem(2, h), sem(2, h), sem(2, b), sem(2, b),
         sem(2, branches, h), sem(2, branches, h), sem(2, h), sem(2, h),
@@ -373,16 +387,28 @@
         jax.ShapeDtypeStruct(branch_keys.shape, F32),
         jax.ShapeDtypeStruct(branch_values.shape, F32),
     )
-    return pl.pallas_call(
+    results = pl.pallas_call(
         functools.partial(kernel, sizes),
         out_shape=outs,
-        in_specs=[vmem, vmem, vmem, whole, whole, whole, whole],
+        in_specs=[whole] * 7,
         out_specs=[vmem] * 6,
         scratch_shapes=scratch,
         compiler_params=pltpu.CompilerParams(
             collective_id=0, has_side_effects=True, vmem_limit_bytes=48 * 1024 * 1024
         ),
-    )(queries, output_cotangent, answer_positions, root_keys, root_values, branch_keys, branch_values)
+    )(*(
+        pltpu.with_memory_space_constraint(array, pltpu.HBM) for array in (
+            queries, output_cotangent, answer_positions, root_keys, root_values,
+            branch_keys, branch_values,
+        )
+    ))
+    return pl.pallas_call(
+        hand_out,
+        out_shape=outs,
+        in_specs=[vmem] * 6,
+        out_specs=[whole] * 6,
+        scratch_shapes=[pltpu.SemaphoreType.DMA((6,))],
+    )(*results)
 
 
 def solution(mesh):

time: 31.3 us -> 28.1 us (0.90)
  local copies, waits for them, and re-layouts: 9.69 us -> 3.99 us
  Pallas kernels: 20.6 us -> 23.2 us
    unnamed x20 -> x12, local copies, waits for them, and re-layouts: 9.69 us -> 3.99 us
    pallas_call x0 -> x1, Pallas kernels: none -> 2.24 us  [per_device(): pl.pallas_call(hand_out, out_shape=outs, in_specs=[vmem] * 6, out_specs=[...]
    pallas_call x1, Pallas kernels: 20.6 us -> 20.9 us  [per_device(): pl.pallas_call(functools.partial(kernel, sizes), out_shape=outs, in_specs...]
where the time goes in v2:
time: 28.1 us; the launch traced here: 27.8 us
  Pallas kernels  23.2 us (83%)
  local copies, waits for them, and re-layouts  3.99 us (14%)
  between operations  0.66 us (2%)
    pallas_call x1, Pallas kernels, per_device(): pl.pallas_call(functools.partial(kernel, sizes), out_shape=outs, in_specs...  20.9 us
    unnamed x12, local copies, waits for them, and re-layouts  3.99 us
    pallas_call x1, Pallas kernels, per_device(): pl.pallas_call(hand_out, out_shape=outs, in_specs=[vmem] * 6, out_specs=[...  2.24 us

profile of v2, /device:TPU:0, one launch (start us, length us, event | category | flops | bytes accessed | tf_op | source)
XLA Modules:
  0.0 27.8 jit_solution(2555761811320740603)
XLA Ops:
  0.6 20.9 %shard_map.118 = (bf16[1,12,4,128]{3,2,1,0:T(4,128)(2,1)S(1)}, f32[1,12,4,128]{3,2,1,0:T(4,128)S(1)}, f32[512,128]{1,0:T(8,128)S(1)}, f32[512,128]{1,0:T(8,128)S...) custom-call(bf16[1,12,4,128]{3,2,1,0:T(4,128)(2,1)} %q_hbm.1, bf16[1,12,4,128]{3,2,1,0:T(4,128)(2,1)} %g_hbm.1, ...), custom_call_target="tpu_custom_call" | custom-call | tf_op jit(solution)/shard_map/pallas_call | solution.py:390
  21.6 0.0 copy-start
  21.6 0.7 %copy-done = f32[512,128]{1,0:T(8,128)} copy-done((f32[512,128]{1,0:T(8,128)}, f32[512,128]{1,0:T(8,128)S(1)}, u32[]{:S(2)}) %copy-start) | copy-done | bytes 262168
  22.3 0.0 copy-start.1
  22.3 0.7 %copy-done.1 = f32[512,128]{1,0:T(8,128)} copy-done((f32[512,128]{1,0:T(8,128)}, f32[512,128]{1,0:T(8,128)S(1)}, u32[]{:S(2)}) %copy-start.1) | copy-done | bytes 262168
  23.0 0.0 copy-start.2
  23.0 0.7 %copy-done.2 = f32[1,512,128]{2,1,0:T(8,128)} copy-done((f32[1,512,128]{2,1,0:T(8,128)}, f32[1,512,128]{2,1,0:T(8,128)S(1)}, u32[]{:S(2)}) %copy-start.2) | copy-done | bytes 262168
  23.7 0.0 copy-start.3
  23.7 0.7 %copy-done.3 = f32[1,512,128]{2,1,0:T(8,128)} copy-done((f32[1,512,128]{2,1,0:T(8,128)}, f32[1,512,128]{2,1,0:T(8,128)S(1)}, u32[]{:S(2)}) %copy-start.3) | copy-done | bytes 262168
  24.4 0.0 copy-start.4
  24.4 0.6 %copy-done.4 = f32[1,12,4,128]{3,2,1,0:T(4,128)} copy-done((f32[1,12,4,128]{3,2,1,0:T(4,128)}, f32[1,12,4,128]{3,2,1,0:T(4,128)S(1)}, u32[]{:S(2)}) %copy-start.4) | copy-done | bytes 24600
  25.0 0.0 copy-start.5
  25.0 0.6 %copy-done.5 = bf16[1,12,4,128]{3,2,1,0:T(4,128)(2,1)} copy-done((bf16[1,12,4,128]{3,2,1,0:T(4,128)(2,1)}, bf16[1,12,4,128]{3,2,1,0:T(4,128)(2,1)S(1)}, u32[]{:S(2)}) %copy-start.5) | copy-done | bytes 12312
  25.6 2.2 %shard_map.119 = (bf16[1,12,4,128]{3,2,1,0:T(4,128)(2,1)}, f32[1,12,4,128]{3,2,1,0:T(4,128)}, f32[512,128]{1,0:T(8,128)}, f32[512,128]{1,0:T(8,128)}, f32[1,512,128]{2,1,0:T(8,128)}, /*index=5*/f32[1,512,128]{2,1,0:T(8,128)}) custom-call(bf16[1,12,4,128]{3,2,1,0:T(4,128)(2,1)} %copy-done.5, f32[1,12,4,128]{3,2,1,0:T(4,128)} %copy-done.4, ...), custom_call_target="tpu_custom_call" | custom-call | tf_op jit(solution)/shard_map/pallas_call | solution.py:405
Async XLA Ops:
  21.6 0.7 %copy-start = (f32[512,128]{1,0:T(8,128)}, f32[512,128]{1,0:T(8,128)S(1)}, u32[]{:S(2)}) copy-start(f32[512,128]{1,0:T(8,128)S(1)} %get-tuple-element.14.refs_2_) | copy-start | bytes 786436
  22.3 0.7 %copy-start.1 = (f32[512,128]{1,0:T(8,128)}, f32[512,128]{1,0:T(8,128)S(1)}, u32[]{:S(2)}) copy-start(f32[512,128]{1,0:T(8,128)S(1)} %get-tuple-element.15.refs_3_) | copy-start | bytes 786436
  23.0 0.7 %copy-start.2 = (f32[1,512,128]{2,1,0:T(8,128)}, f32[1,512,128]{2,1,0:T(8,128)S(1)}, u32[]{:S(2)}) copy-start(f32[1,512,128]{2,1,0:T(8,128)S(1)} %get-tuple-element.16.refs_4_) | copy-start | bytes 786436
  23.7 0.7 %copy-start.3 = (f32[1,512,128]{2,1,0:T(8,128)}, f32[1,512,128]{2,1,0:T(8,128)S(1)}, u32[]{:S(2)}) copy-start(f32[1,512,128]{2,1,0:T(8,128)S(1)} %get-tuple-element.17.refs_5_) | copy-start | bytes 786436
  24.4 0.6 %copy-start.4 = (f32[1,12,4,128]{3,2,1,0:T(4,128)}, f32[1,12,4,128]{3,2,1,0:T(4,128)S(1)}, u32[]{:S(2)}) copy-start(f32[1,12,4,128]{3,2,1,0:T(4,128)S(1)} %get-tuple-element.13.refs_1_) | copy-start | bytes 73732
  25.0 0.6 %copy-start.5 = (bf16[1,12,4,128]{3,2,1,0:T(4,128)(2,1)}, bf16[1,12,4,128]{3,2,1,0:T(4,128)(2,1)S(1)}, u32[]{:S(2)}) copy-start(bf16[1,12,4,128]{3,2,1,0:T(4,128)(2,1)S(1)} %get-tuple-element.12.refs_0_) | copy-start | bytes 36868

commit v3 on v2

--- a/solution.py
+++ b/solution.py
@@ -48,7 +48,7 @@
     sizes,
     q_hbm, g_hbm, pos_hbm, rk_hbm, rv_hbm, bk_hbm, bv_hbm,
     att_out, dq_out, rk_out, rv_out, bk_out, bv_out,
-    rows_in, pos_ref, keys, values, rows_f32, qbuf, gbuf, stats, probs, product, weighted, place,
+    pos_ref, keys, values, rows_f32, qbuf, gbuf, stats, probs, product, weighted, place,
     att_send, att_recv, dq_acc, dq_send, dq_recv,
     root_part, root_recv, root_all, branch_all, slope_root, slope_branch, grads,
     load_sem, q_ss, q_rs, g_ss, g_rs, st_ss, st_rs, at_ss, at_rs, dq_ss, dq_rs,
@@ -58,8 +58,8 @@
     me, my_head, my_branch = (
         lax.axis_index("seq"), lax.axis_index("head"), lax.axis_index("branch")
     )
-    answers, per, width = q_hbm.shape[1:]
-    own = answers * per
+    own, width = q_hbm.shape
+    answers, per = att_out.shape[1:3]
     padded = qbuf.shape[0]
     chunks = padded // ROWS
     root_rows, branch_rows = rk_hbm.shape[0], bk_hbm.shape[1]
@@ -91,9 +91,10 @@
                 barrier, inc=1, device_id=to(d), device_id_type=pl.DeviceIdType.MESH
             )
 
+    mine = pl.ds(pl.multiple_of(me * own, 16), own)
     loads = [
-        pltpu.make_async_copy(q_hbm.at[0], rows_in.at[0], load_sem.at[4]),
-        pltpu.make_async_copy(g_hbm.at[0], rows_in.at[1], load_sem.at[5]),
+        pltpu.make_async_copy(q_hbm, qbuf.at[mine], load_sem.at[4]),
+        pltpu.make_async_copy(g_hbm, gbuf.at[mine], load_sem.at[5]),
         pltpu.make_async_copy(pos_hbm, pos_ref, load_sem.at[6]),
         pltpu.make_async_copy(rk_hbm, keys.at[pl.ds(0, root_rows)], load_sem.at[0]),
         pltpu.make_async_copy(bk_hbm.at[0], keys.at[pl.ds(root_rows, branch_rows)], load_sem.at[1]),
@@ -103,13 +104,8 @@
     for load in loads:
         load.start()
 
-    mine = pl.ds(pl.multiple_of(me * own, 16), own)
-    for at, target in enumerate((qbuf, gbuf)):
-        loads[at].wait()
-        for i in range(answers):
-            rows_f32[at, i * per:(i + 1) * per, :] = rows_in[at, i].astype(F32)
-        target[mine, :] = rows_f32[at].astype(BF16)
-        if padded > n * own:
+    if padded > n * own:
+        for target in (qbuf, gbuf):
             target[n * own:, :] = jnp.zeros((padded - n * own, width), BF16)
 
     pl.semaphore_wait(barrier, (n - 1) + (heads - 1) + (branches - 1))
@@ -121,9 +117,9 @@
         copy.start()
         sends.append(copy)
 
-    for buf, ss, rs in ((qbuf, q_ss, q_rs), (gbuf, g_ss, g_rs)):
+    for rows, buf, ss, rs in ((q_hbm, qbuf, q_ss, q_rs), (g_hbm, gbuf, g_ss, g_rs)):
         for d in range(1, n):
-            send(buf.at[mine], buf.at[mine], ss.at[d - 1], rs.at[d - 1], seq_to(d))
+            send(rows, buf.at[mine], ss.at[d - 1], rs.at[d - 1], seq_to(d))
 
     def arrived_rows(buf, ss, rs):
         for d in range(1, n):
@@ -145,7 +141,7 @@
 
     over(chunks, expand)
 
-    for load in loads[3:]:
+    for load in loads[:2] + loads[3:]:
         load.wait()
     arrived_rows(qbuf, q_ss, q_rs)
 
@@ -265,6 +261,15 @@
         for d in range(1, heads):
             send(block, block, br_ss.at[at, d - 1], br_rs.at[at, d - 1], head_to(d))
 
+    def forward(at):
+        for d in range(1, branches):
+            block = root_all.at[at, branch_from(d), my_head]
+            remote(block, block, x_ss.at[at, d - 1], x_rs.at[at, d - 1], branch_to(d)).wait_recv()
+            for e in range(1, heads):
+                send(block, block, hd_ss.at[at, d, e - 1], hd_rs.at[at, d, e - 1], head_to(e))
+
+    forward(0)
+
     def query_terms(c):
         term = dot_first(slope_root[c], keys[:root_rows, :])
         term = term + dot_first(slope_branch[c], keys[root_rows:, :])
@@ -277,12 +282,7 @@
             far = pl.ds(pl.multiple_of(lax.rem(me + d, n) * own, 16), own)
             send(buf.at[far], into.at[d - 1], ss.at[d - 1], rs.at[d - 1], seq_to(d))
 
-    for at in range(2):
-        for d in range(1, branches):
-            block = root_all.at[at, branch_from(d), my_head]
-            remote(block, block, x_ss.at[at, d - 1], x_rs.at[at, d - 1], branch_to(d)).wait_recv()
-            for e in range(1, heads):
-                send(block, block, hd_ss.at[at, d, e - 1], hd_rs.at[at, d, e - 1], head_to(e))
+    forward(1)
 
     for at, out in ((0, bv_out), (1, bk_out)):
         for d in range(1, heads):
@@ -350,7 +350,6 @@
 
     z, h, b = max(1, n - 1), max(1, heads - 1), max(1, branches - 1)
     scratch = [
-        pltpu.VMEM((2, answers, per, width), BF16),
         pltpu.VMEM(answer_positions.shape, jnp.int32),
         pltpu.VMEM((key_rows, width), BF16),
         pltpu.VMEM((key_rows, width), BF16),
@@ -398,7 +397,8 @@
         ),
     )(*(
         pltpu.with_memory_space_constraint(array, pltpu.HBM) for array in (
-            queries, output_cotangent, answer_positions, root_keys, root_values,
+            queries.reshape(own, width), output_cotangent.reshape(own, width),
+            answer_positions, root_keys, root_values,
             branch_keys, branch_values,
         )
     ))
@@ -408,6 +408,7 @@
         in_specs=[vmem] * 6,
         out_specs=[whole] * 6,
         scratch_shapes=[pltpu.SemaphoreType.DMA((6,))],
+        compiler_params=pltpu.CompilerParams(vmem_limit_bytes=2 * 1024 * 1024),
     )(*results)
 
 

time: 28.1 us -> 25.2 us (0.90)
  local copies, waits for them, and re-layouts: 3.99 us -> 0 us
  Pallas kernels: 23.2 us -> 24.4 us
    unnamed x12 -> x0, local copies, waits for them, and re-layouts: 3.99 us -> none
    pallas_call x1, Pallas kernels: 20.9 us -> 23.4 us  [per_device(): pl.pallas_call(functools.partial(kernel, sizes), out_shape=outs, in_specs...]
    pallas_call x1, Pallas kernels: 2.24 us -> 1.03 us  [per_device(): pl.pallas_call(hand_out, out_shape=outs, in_specs=[vmem] * 6, out_specs=[...]
where the time goes in v3:
time: 25.2 us; the launch traced here: 25.1 us
  Pallas kernels  24.4 us (97%)
  between operations  0.64 us (3%)
    pallas_call x1, Pallas kernels, per_device(): pl.pallas_call(functools.partial(kernel, sizes), out_shape=outs, in_specs...  23.4 us
    pallas_call x1, Pallas kernels, per_device(): pl.pallas_call(hand_out, out_shape=outs, in_specs=[vmem] * 6, out_specs=[...  1.03 us

profile of v3, /device:TPU:0, one launch (start us, length us, event | category | flops | bytes accessed | tf_op | source)
XLA Modules:
  0.0 25.1 jit_solution(7153464070027847636)
XLA Ops:
  0.6 23.4 %shard_map.118 = (bf16[1,12,4,128]{3,2,1,0:T(4,128)(2,1)S(1)}, f32[1,12,4,128]{3,2,1,0:T(4,128)S(1)}, f32[512,128]{1,0:T(8,128)S(1)}, f32[512,128]{1,0:T(8,128)S...) custom-call(bf16[48,128]{1,0:T(8,128)(2,1)} %bitcast.2, bf16[48,128]{1,0:T(8,128)(2,1)} %bitcast.3, ...), custom_call_target="tpu_custom_call" | custom-call | tf_op jit(solution)/shard_map/pallas_call | solution.py:389
  24.1 1.0 %shard_map.119 = (bf16[1,12,4,128]{3,2,1,0:T(4,128)(2,1)}, f32[1,12,4,128]{3,2,1,0:T(4,128)}, f32[512,128]{1,0:T(8,128)}, f32[512,128]{1,0:T(8,128)}, f32[1,512,128]{2,1,0:T(8,128)}, /*index=5*/f32[1,512,128]{2,1,0:T(8,128)}) custom-call(bf16[1,12,4,128]{3,2,1,0:T(4,128)(2,1)S(1)} %get-tuple-element.12.refs_0_, ...), custom_call_target="tpu_custom_call" | custom-call | tf_op jit(solution)/shard_map/pallas_call | solution.py:405

commit v4 on v3

--- a/solution.py
+++ b/solution.py
@@ -16,10 +16,6 @@
 
 def dot_last(left, right):
     return lax.dot_general(left, right, (((1,), (1,)), ((), ())), preferred_element_type=F32)
-
-
-def dot_first(left, right):
-    return lax.dot_general(left, right, (((0,), (0,)), ((), ())), preferred_element_type=F32)
 
 
 def dot_plain(left, right):
@@ -48,9 +44,9 @@
     sizes,
     q_hbm, g_hbm, pos_hbm, rk_hbm, rv_hbm, bk_hbm, bv_hbm,
     att_out, dq_out, rk_out, rv_out, bk_out, bv_out,
-    pos_ref, keys, values, rows_f32, qbuf, gbuf, stats, probs, product, weighted, place,
-    att_send, att_recv, dq_acc, dq_send, dq_recv,
-    root_part, root_recv, root_all, branch_all, slope_root, slope_branch, grads,
+    pos_ref, keys, values, keys_t, values_t, rows_f32, qbuf, gbuf, stats, probs, product, weighted, place,
+    att_send, att_recv, near, dq_send, dq_recv,
+    root_part, root_recv, root_all, branch_all, slope, grads,
     load_sem, q_ss, q_rs, g_ss, g_rs, st_ss, st_rs, at_ss, at_rs, dq_ss, dq_rs,
     rs_ss, rs_rs, x_ss, x_rs, hd_ss, hd_rs, br_ss, br_rs,
 ):
@@ -92,6 +88,19 @@
             )
 
     mine = pl.ds(pl.multiple_of(me * own, 16), own)
+    pl.semaphore_wait(barrier, (n - 1) + (heads - 1) + (branches - 1))
+
+    sends = []
+
+    def send(*pieces):
+        copy = remote(*pieces)
+        copy.start()
+        sends.append(copy)
+
+    for rows, buf, ss, rs in ((q_hbm, qbuf, q_ss, q_rs), (g_hbm, gbuf, g_ss, g_rs)):
+        for d in range(1, n):
+            send(rows, buf.at[mine], ss.at[d - 1], rs.at[d - 1], seq_to(d))
+
     loads = [
         pltpu.make_async_copy(q_hbm, qbuf.at[mine], load_sem.at[4]),
         pltpu.make_async_copy(g_hbm, gbuf.at[mine], load_sem.at[5]),
@@ -108,19 +117,6 @@
         for target in (qbuf, gbuf):
             target[n * own:, :] = jnp.zeros((padded - n * own, width), BF16)
 
-    pl.semaphore_wait(barrier, (n - 1) + (heads - 1) + (branches - 1))
-
-    sends = []
-
-    def send(*pieces):
-        copy = remote(*pieces)
-        copy.start()
-        sends.append(copy)
-
-    for rows, buf, ss, rs in ((q_hbm, qbuf, q_ss, q_rs), (g_hbm, gbuf, g_ss, g_rs)):
-        for d in range(1, n):
-            send(rows, buf.at[mine], ss.at[d - 1], rs.at[d - 1], seq_to(d))
-
     def arrived_rows(buf, ss, rs):
         for d in range(1, n):
             rows = pl.ds(pl.multiple_of(seq_from(d) * own, 16), own)
@@ -141,7 +137,11 @@
 
     over(chunks, expand)
 
-    for load in loads[:2] + loads[3:]:
+    for load in loads[3:]:
+        load.wait()
+    keys_t[...] = keys[...].astype(F32).T.astype(BF16)
+    values_t[...] = values[...].astype(F32).T.astype(BF16)
+    for load in loads[:2]:
         load.wait()
     arrived_rows(qbuf, q_ss, q_rs)
 
@@ -165,8 +165,8 @@
         probs[c, :root_rows, :] = p_root
         probs[c, root_rows:, :] = p_branch
         sums = jnp.sum(p_root, axis=0, keepdims=True) + jnp.sum(p_branch, axis=0, keepdims=True)
-        share = dot_first(values[:root_rows, :], p_root.astype(BF16))
-        share = share + dot_first(values[root_rows:, :], p_branch.astype(BF16))
+        share = dot_plain(values_t[:, :root_rows], p_root.astype(BF16))
+        share = share + dot_plain(values_t[:, root_rows:], p_branch.astype(BF16))
         weighted[c] = share
         stats[me, c, 0:1, :] = peak
         stats[me, c, 1:2, :] = sums
@@ -208,40 +208,45 @@
 
     over(chunks, combine)
 
-    def value_term(c, start, count, slope):
-        weights = probs[c, start:start + count, :] * place[c, 1:2, :]
+    def value_term(c, span):
+        weights = probs[c, span, :] * place[c, 1:2, :]
         return dot_plain(weights.astype(BF16), gbuf[rows_of(c), :])
 
-    def key_term(c, start, count, slope):
-        weights = probs[c, start:start + count, :] * place[c, 1:2, :]
-        gap = product[c, start:start + count, :] - place[c, 2:3, :]
+    def key_term(c, span):
+        weights = probs[c, span, :] * place[c, 1:2, :]
+        gap = product[c, span, :] - place[c, 2:3, :]
         sloped = (weights * gap).astype(BF16)
-        slope[c] = sloped
+        slope[c, span, :] = sloped
         return dot_plain(sloped, qbuf[rows_of(c), :]) * scale
 
-    def sweep(term, start, count, slope):
+    def sweep(term, start, count):
+        span = pl.ds(start, count)
         if chunks == 1:
-            return term(0, start, count, slope)
+            return term(0, span)
         grads[:count, :] = jnp.zeros((count, width), F32)
 
         def add(c):
-            grads[:count, :] += term(c, start, count, slope)
+            grads[:count, :] += term(c, span)
 
         over(chunks, add)
         return grads[:count, :]
 
-    for at, term in enumerate((value_term, key_term)):
-        root_part[at] = sweep(term, 0, root_rows, slope_root).astype(BF16)
+    def piece_start(d):
+        return pl.multiple_of(lax.rem(my_head + d, heads) * piece, 16)
+
+    def far_pieces(at, term):
         for d in range(1, heads):
-            far = pl.ds(pl.multiple_of(lax.rem(my_head + d, heads) * piece, 16), piece)
+            root_part[at, d - 1] = sweep(term, piece_start(d), piece).astype(BF16)
             send(
-                root_part.at[at, far], root_recv.at[at, d - 1],
+                root_part.at[at, d - 1], root_recv.at[at, d - 1],
                 rs_ss.at[at, d - 1], rs_rs.at[at, d - 1], head_to(d),
             )
 
-    near = pl.ds(pl.multiple_of(my_head * piece, 16), piece)
-    for at in range(2):
-        term = root_part[at, near, :].astype(F32)
+    def near_piece(at, term):
+        near[at] = sweep(term, piece_start(0), piece)
+
+    def spread(at):
+        term = near[at]
         for d in range(1, heads):
             remote(
                 root_recv.at[at, d - 1], root_recv.at[at, d - 1],
@@ -255,11 +260,35 @@
         for d in range(1, heads):
             send(block, block, hd_ss.at[at, 0, d - 1], hd_rs.at[at, 0, d - 1], head_to(d))
 
+    far_pieces(0, value_term)
+    near_piece(0, value_term)
+    far_pieces(1, key_term)
+    spread(0)
+    near_piece(1, key_term)
+    spread(1)
+
     for at, term in enumerate((value_term, key_term)):
-        branch_all[at, my_head] = sweep(term, root_rows, branch_rows, slope_branch).astype(BF16)
+        branch_all[at, my_head] = sweep(term, root_rows, branch_rows).astype(BF16)
         block = branch_all.at[at, my_head]
         for d in range(1, heads):
             send(block, block, br_ss.at[at, d - 1], br_rs.at[at, d - 1], head_to(d))
+
+    def share_rows(buf, into, ss, rs):
+        for d in range(1, n):
+            far = pl.ds(pl.multiple_of(lax.rem(me + d, n) * own, 16), own)
+            send(buf.at[far], into.at[d - 1], ss.at[d - 1], rs.at[d - 1], seq_to(d))
+
+    def query_terms(c):
+        term = dot_plain(keys_t[...], slope[c]) * scale
+        dq_send[rows_of(c), :] = term.T.astype(BF16)
+
+    def shares(c):
+        att_send[rows_of(c), :] = (weighted[c] * place[c, 1:2, :]).T.astype(BF16)
+
+    over(chunks, query_terms)
+    share_rows(dq_send, dq_recv, dq_ss, dq_rs)
+    over(chunks, shares)
+    share_rows(att_send, att_recv, at_ss, at_rs)
 
     def forward(at):
         for d in range(1, branches):
@@ -267,22 +296,6 @@
             remote(block, block, x_ss.at[at, d - 1], x_rs.at[at, d - 1], branch_to(d)).wait_recv()
             for e in range(1, heads):
                 send(block, block, hd_ss.at[at, d, e - 1], hd_rs.at[at, d, e - 1], head_to(e))
-
-    forward(0)
-
-    def query_terms(c):
-        term = dot_first(slope_root[c], keys[:root_rows, :])
-        term = term + dot_first(slope_branch[c], keys[root_rows:, :])
-        dq_send[rows_of(c), :] = (term * scale).astype(BF16)
-        att_send[rows_of(c), :] = (weighted[c] * place[c, 1:2, :]).T.astype(BF16)
-
-    over(chunks, query_terms)
-    for buf, into, ss, rs in ((dq_send, dq_recv, dq_ss, dq_rs), (att_send, att_recv, at_ss, at_rs)):
-        for d in range(1, n):
-            far = pl.ds(pl.multiple_of(lax.rem(me + d, n) * own, 16), own)
-            send(buf.at[far], into.at[d - 1], ss.at[d - 1], rs.at[d - 1], seq_to(d))
-
-    forward(1)
 
     for at, out in ((0, bv_out), (1, bk_out)):
         for d in range(1, heads):
@@ -292,6 +305,9 @@
         for h in range(1, heads):
             term = term + branch_all[at, h].astype(F32)
         out[0] = term
+
+    forward(0)
+    forward(1)
 
     for at, (buf, into, ss, rs, out) in enumerate((
         (dq_send, dq_recv, dq_ss, dq_rs, dq_out), (att_send, att_recv, at_ss, at_rs, att_out)
@@ -353,6 +369,8 @@
         pltpu.VMEM(answer_positions.shape, jnp.int32),
         pltpu.VMEM((key_rows, width), BF16),
         pltpu.VMEM((key_rows, width), BF16),
+        pltpu.VMEM((width, key_rows), BF16),
+        pltpu.VMEM((width, key_rows), BF16),
         pltpu.VMEM((2, own, width), F32),
         pltpu.VMEM((padded, width), BF16),
         pltpu.VMEM((padded, width), BF16),
@@ -363,15 +381,14 @@
         pltpu.VMEM((chunks, 8, ROWS), F32),
         pltpu.VMEM((padded, width), BF16),
         pltpu.VMEM((z, own, width), BF16),
-        pltpu.VMEM((8, 128), F32),
+        pltpu.VMEM((2, piece, width), F32),
         pltpu.VMEM((padded, width), BF16),
         pltpu.VMEM((z, own, width), BF16),
-        pltpu.VMEM((2, root_rows, width), BF16),
+        pltpu.VMEM((2, h, piece, width), BF16),
         pltpu.VMEM((2, h, piece, width), BF16),
         pltpu.VMEM((2, branches, heads, piece, width), BF16),
         pltpu.VMEM((2, heads, branch_rows, width), BF16),
-        pltpu.VMEM((chunks, root_rows, ROWS), BF16),
-        pltpu.VMEM((chunks, branch_rows, ROWS), BF16),
+        pltpu.VMEM((chunks, key_rows, ROWS), BF16),
         pltpu.VMEM((max(root_rows, branch_rows), width), F32),
         sem(7),
         sem(z), sem(z), sem(z), sem(z), sem(z), sem(z), sem(z), sem(z), sem(z), sem(z),

time: 25.2 us -> 22.9 us (0.909)
  Pallas kernels: 24.4 us -> 22.1 us
    pallas_call x1, Pallas kernels: 23.4 us -> 21.1 us  [per_device(): pl.pallas_call(functools.partial(kernel, sizes), out_shape=outs, in_specs...]
where the time goes in v4:
time: 22.9 us; the launch traced here: 22.7 us
  Pallas kernels  22.1 us (97%)
  between operations  0.64 us (3%)
    pallas_call x1, Pallas kernels, per_device(): pl.pallas_call(functools.partial(kernel, sizes), out_shape=outs, in_specs...  21.1 us
    pallas_call x1, Pallas kernels, per_device(): pl.pallas_call(hand_out, out_shape=outs, in_specs=[vmem] * 6, out_specs=[...  1.03 us

profile of v4, /device:TPU:0, one launch (start us, length us, event | category | flops | bytes accessed | tf_op | source)
XLA Modules:
  0.0 22.7 jit_solution(2806126867567991264)
XLA Ops:
  0.6 21.1 %shard_map.118 = (bf16[1,12,4,128]{3,2,1,0:T(4,128)(2,1)S(1)}, f32[1,12,4,128]{3,2,1,0:T(4,128)S(1)}, f32[512,128]{1,0:T(8,128)S(1)}, f32[512,128]{1,0:T(8,128)S...) custom-call(bf16[48,128]{1,0:T(8,128)(2,1)} %bitcast.2, bf16[48,128]{1,0:T(8,128)(2,1)} %bitcast.3, ...), custom_call_target="tpu_custom_call" | custom-call | tf_op jit(solution)/shard_map/pallas_call | solution.py:406
  21.7 1.0 %shard_map.119 = (bf16[1,12,4,128]{3,2,1,0:T(4,128)(2,1)}, f32[1,12,4,128]{3,2,1,0:T(4,128)}, f32[512,128]{1,0:T(8,128)}, f32[512,128]{1,0:T(8,128)}, f32[1,512,128]{2,1,0:T(8,128)}, /*index=5*/f32[1,512,128]{2,1,0:T(8,128)}) custom-call(bf16[1,12,4,128]{3,2,1,0:T(4,128)(2,1)S(1)} %get-tuple-element.12.refs_0_, ...), custom_call_target="tpu_custom_call" | custom-call | tf_op jit(solution)/shard_map/pallas_call | solution.py:422

commit v5 on v4

--- a/solution.py
+++ b/solution.py
@@ -88,19 +88,6 @@
             )
 
     mine = pl.ds(pl.multiple_of(me * own, 16), own)
-    pl.semaphore_wait(barrier, (n - 1) + (heads - 1) + (branches - 1))
-
-    sends = []
-
-    def send(*pieces):
-        copy = remote(*pieces)
-        copy.start()
-        sends.append(copy)
-
-    for rows, buf, ss, rs in ((q_hbm, qbuf, q_ss, q_rs), (g_hbm, gbuf, g_ss, g_rs)):
-        for d in range(1, n):
-            send(rows, buf.at[mine], ss.at[d - 1], rs.at[d - 1], seq_to(d))
-
     loads = [
         pltpu.make_async_copy(q_hbm, qbuf.at[mine], load_sem.at[4]),
         pltpu.make_async_copy(g_hbm, gbuf.at[mine], load_sem.at[5]),
@@ -113,6 +100,20 @@
     for load in loads:
         load.start()
 
+    pl.semaphore_wait(barrier, (n - 1) + (heads - 1) + (branches - 1))
+
+    sends = []
+
+    def send(*pieces):
+        copy = remote(*pieces)
+        copy.start()
+        sends.append(copy)
+
+    for load, buf, ss, rs in ((loads[0], qbuf, q_ss, q_rs), (loads[1], gbuf, g_ss, g_rs)):
+        load.wait()
+        for d in range(1, n):
+            send(buf.at[mine], buf.at[mine], ss.at[d - 1], rs.at[d - 1], seq_to(d))
+
     if padded > n * own:
         for target in (qbuf, gbuf):
             target[n * own:, :] = jnp.zeros((padded - n * own, width), BF16)
@@ -139,10 +140,7 @@
 
     for load in loads[3:]:
         load.wait()
-    keys_t[...] = keys[...].astype(F32).T.astype(BF16)
     values_t[...] = values[...].astype(F32).T.astype(BF16)
-    for load in loads[:2]:
-        load.wait()
     arrived_rows(qbuf, q_ss, q_rs)
 
     key_place = (
@@ -189,6 +187,7 @@
         product[c, root_rows:, :] = dot_last(values[root_rows:, :], g)
 
     over(chunks, products)
+    keys_t[...] = keys[...].astype(F32).T.astype(BF16)
     for d in range(1, n):
         at = seq_from(d)
         remote(stats.at[at], stats.at[at], st_ss.at[d - 1], st_rs.at[d - 1], seq_to(d)).wait_recv()

time: 22.9 us -> 22.7 us (level)
  no operation moved by 1% of the time
where the time goes in v5:
time: 22.7 us; the launch traced here: 22.5 us
  Pallas kernels  21.9 us (96%)
  between operations  0.64 us (3%)
    pallas_call x1, Pallas kernels, per_device(): pl.pallas_call(functools.partial(kernel, sizes), out_shape=outs, in_specs...  20.9 us
    pallas_call x1, Pallas kernels, per_device(): pl.pallas_call(hand_out, out_shape=outs, in_specs=[vmem] * 6, out_specs=[...  1.03 us

profile of v5, /device:TPU:0, one launch (start us, length us, event | category | flops | bytes accessed | tf_op | source)
XLA Modules:
  0.0 22.5 jit_solution(7864512193362470015)
XLA Ops:
  0.6 20.9 %shard_map.118 = (bf16[1,12,4,128]{3,2,1,0:T(4,128)(2,1)S(1)}, f32[1,12,4,128]{3,2,1,0:T(4,128)S(1)}, f32[512,128]{1,0:T(8,128)S(1)}, f32[512,128]{1,0:T(8,128)S...) custom-call(bf16[48,128]{1,0:T(8,128)(2,1)} %bitcast.2, bf16[48,128]{1,0:T(8,128)(2,1)} %bitcast.3, ...), custom_call_target="tpu_custom_call" | custom-call | tf_op jit(solution)/shard_map/pallas_call | solution.py:405
  21.5 1.0 %shard_map.119 = (bf16[1,12,4,128]{3,2,1,0:T(4,128)(2,1)}, f32[1,12,4,128]{3,2,1,0:T(4,128)}, f32[512,128]{1,0:T(8,128)}, f32[512,128]{1,0:T(8,128)}, f32[1,512,128]{2,1,0:T(8,128)}, /*index=5*/f32[1,512,128]{2,1,0:T(8,128)}) custom-call(bf16[1,12,4,128]{3,2,1,0:T(4,128)(2,1)S(1)} %get-tuple-element.12.refs_0_, ...), custom_call_target="tpu_custom_call" | custom-call | tf_op jit(solution)/shard_map/pallas_call | solution.py:421

commit v6 on v5

--- a/solution.py
+++ b/solution.py
@@ -45,10 +45,10 @@
     q_hbm, g_hbm, pos_hbm, rk_hbm, rv_hbm, bk_hbm, bv_hbm,
     att_out, dq_out, rk_out, rv_out, bk_out, bv_out,
     pos_ref, keys, values, keys_t, values_t, rows_f32, qbuf, gbuf, stats, probs, product, weighted, place,
-    att_send, att_recv, near, dq_send, dq_recv,
-    root_part, root_recv, root_all, branch_all, slope, grads,
+    att_send, att_recv, dq_send, dq_recv,
+    q_far, g_far, place_far, terms, root_all, branch_all, slope, grads,
     load_sem, q_ss, q_rs, g_ss, g_rs, st_ss, st_rs, at_ss, at_rs, dq_ss, dq_rs,
-    rs_ss, rs_rs, x_ss, x_rs, hd_ss, hd_rs, br_ss, br_rs,
+    rs_ss, rs_rs, x_ss, x_rs, xq_ss, xq_rs, xg_ss, xg_rs, br_ss, br_rs,
 ):
     n, heads, branches = sizes
     me, my_head, my_branch = (
@@ -59,7 +59,6 @@
     padded = qbuf.shape[0]
     chunks = padded // ROWS
     root_rows, branch_rows = rk_hbm.shape[0], bk_hbm.shape[1]
-    piece = root_rows // heads
     scale = 1.0 / math.sqrt(width)
 
     def seq_to(d):
@@ -114,14 +113,26 @@
         for d in range(1, n):
             send(buf.at[mine], buf.at[mine], ss.at[d - 1], rs.at[d - 1], seq_to(d))
 
+    def across(buf, far, ss, rs, d):
+        rows = pl.ds(pl.multiple_of(seq_from(d) * own, 16), own)
+        for e in range(1, branches):
+            send(buf.at[rows], far.at[e - 1, rows], ss.at[e - 1, d], rs.at[e - 1, d], branch_to(e))
+
+    across(qbuf, q_far, xq_ss, xq_rs, 0)
+    across(gbuf, g_far, xg_ss, xg_rs, 0)
+
     if padded > n * own:
         for target in (qbuf, gbuf):
             target[n * own:, :] = jnp.zeros((padded - n * own, width), BF16)
-
-    def arrived_rows(buf, ss, rs):
+        for target in (q_far, g_far):
+            for e in range(1, branches):
+                target[e - 1, n * own:, :] = jnp.zeros((padded - n * own, width), BF16)
+
+    def arrived_rows(buf, ss, rs, far, far_ss, far_rs):
         for d in range(1, n):
             rows = pl.ds(pl.multiple_of(seq_from(d) * own, 16), own)
             remote(buf.at[rows], buf.at[rows], ss.at[d - 1], rs.at[d - 1], seq_to(d)).wait_recv()
+            across(buf, far, far_ss, far_rs, d)
 
     loads[2].wait()
     total = pos_ref.shape[1]
@@ -141,7 +152,7 @@
     for load in loads[3:]:
         load.wait()
     values_t[...] = values[...].astype(F32).T.astype(BF16)
-    arrived_rows(qbuf, q_ss, q_rs)
+    arrived_rows(qbuf, q_ss, q_rs, q_far, xq_ss, xq_rs)
 
     key_place = (
         lax.broadcasted_iota(jnp.int32, (branch_rows, ROWS), 0) + me * branch_rows
@@ -160,7 +171,7 @@
         )
         p_root = jnp.exp(on_root - peak)
         p_branch = jnp.exp(on_branch - peak)
-        probs[c, :root_rows, :] = p_root
+        probs[c, :root_rows, :] = on_root
         probs[c, root_rows:, :] = p_branch
         sums = jnp.sum(p_root, axis=0, keepdims=True) + jnp.sum(p_branch, axis=0, keepdims=True)
         share = dot_plain(values_t[:, :root_rows], p_root.astype(BF16))
@@ -170,7 +181,7 @@
         stats[me, c, 1:2, :] = sums
 
     over(chunks, scores)
-    arrived_rows(gbuf, g_ss, g_rs)
+    arrived_rows(gbuf, g_ss, g_rs, g_far, xg_ss, xg_rs)
 
     def dots(c):
         turned = gbuf[rows_of(c), :].astype(F32).T
@@ -204,73 +215,78 @@
         factor = jnp.exp(stats[me, c, 0:1, :] - peak) / sums
         place[c, 1:2, :] = factor
         place[c, 2:3, :] = dotted / sums
+        place[c, 3:4, :] = peak
+        place[c, 4:5, :] = 1.0 / sums
 
     over(chunks, combine)
 
-    def value_term(c, span):
-        weights = probs[c, span, :] * place[c, 1:2, :]
+    for e in range(1, branches):
+        send(place, place_far.at[e - 1], x_ss.at[e - 1], x_rs.at[e - 1], branch_to(e))
+
+    def root_weights(score, norm):
+        return jnp.exp(score - norm[3:4, :]) * norm[4:5, :]
+
+    def root_value_term(score, norm, g):
+        return dot_plain(root_weights(score, norm).astype(BF16), g)
+
+    def root_key_term(score, gap, norm, q):
+        sloped = (root_weights(score, norm) * (gap - norm[2:3, :])).astype(BF16)
+        return sloped, dot_plain(sloped, q) * scale
+
+    def put(at, branch, c, term):
+        if chunks == 1:
+            terms[at, branch] = term
+            return
+        kept = jnp.where(c == 0, 0.0, terms[at, branch])
+        terms[at, branch] = kept + term
+
+    def own_root(c):
+        score, norm = probs[c, :root_rows, :], place[c]
+        put(0, my_branch, c, root_value_term(score, norm, gbuf[rows_of(c), :]))
+        sloped, term = root_key_term(score, product[c, :root_rows, :], norm, qbuf[rows_of(c), :])
+        slope[c, :root_rows, :] = sloped
+        put(1, my_branch, c, term)
+
+    def branch_value_term(c):
+        weights = probs[c, root_rows:, :] * place[c, 1:2, :]
         return dot_plain(weights.astype(BF16), gbuf[rows_of(c), :])
 
-    def key_term(c, span):
-        weights = probs[c, span, :] * place[c, 1:2, :]
-        gap = product[c, span, :] - place[c, 2:3, :]
+    def branch_key_term(c):
+        weights = probs[c, root_rows:, :] * place[c, 1:2, :]
+        gap = product[c, root_rows:, :] - place[c, 2:3, :]
         sloped = (weights * gap).astype(BF16)
-        slope[c, span, :] = sloped
+        slope[c, root_rows:, :] = sloped
         return dot_plain(sloped, qbuf[rows_of(c), :]) * scale
 
-    def sweep(term, start, count):
-        span = pl.ds(start, count)
+    def sweep(term, count):
         if chunks == 1:
-            return term(0, span)
+            return term(0)
         grads[:count, :] = jnp.zeros((count, width), F32)
 
         def add(c):
-            grads[:count, :] += term(c, span)
+            grads[:count, :] += term(c)
 
         over(chunks, add)
         return grads[:count, :]
 
-    def piece_start(d):
-        return pl.multiple_of(lax.rem(my_head + d, heads) * piece, 16)
-
-    def far_pieces(at, term):
+    def to_heads(buf, at, term, ss, rs):
+        buf[at, my_head] = term.astype(BF16)
+        block = buf.at[at, my_head]
         for d in range(1, heads):
-            root_part[at, d - 1] = sweep(term, piece_start(d), piece).astype(BF16)
-            send(
-                root_part.at[at, d - 1], root_recv.at[at, d - 1],
-                rs_ss.at[at, d - 1], rs_rs.at[at, d - 1], head_to(d),
-            )
-
-    def near_piece(at, term):
-        near[at] = sweep(term, piece_start(0), piece)
-
-    def spread(at):
-        term = near[at]
+            send(block, block, ss.at[at, d - 1], rs.at[at, d - 1], head_to(d))
+
+    def from_heads(buf, at, ss, rs):
         for d in range(1, heads):
-            remote(
-                root_recv.at[at, d - 1], root_recv.at[at, d - 1],
-                rs_ss.at[at, d - 1], rs_rs.at[at, d - 1], head_to(d),
-            ).wait_recv()
-            term = term + root_recv[at, d - 1].astype(F32)
-        root_all[at, my_branch, my_head] = term.astype(BF16)
-        block = root_all.at[at, my_branch, my_head]
-        for d in range(1, branches):
-            send(block, block, x_ss.at[at, d - 1], x_rs.at[at, d - 1], branch_to(d))
-        for d in range(1, heads):
-            send(block, block, hd_ss.at[at, 0, d - 1], hd_rs.at[at, 0, d - 1], head_to(d))
-
-    far_pieces(0, value_term)
-    near_piece(0, value_term)
-    far_pieces(1, key_term)
-    spread(0)
-    near_piece(1, key_term)
-    spread(1)
-
-    for at, term in enumerate((value_term, key_term)):
-        branch_all[at, my_head] = sweep(term, root_rows, branch_rows).astype(BF16)
-        block = branch_all.at[at, my_head]
-        for d in range(1, heads):
-            send(block, block, br_ss.at[at, d - 1], br_rs.at[at, d - 1], head_to(d))
+            block = buf.at[at, head_from(d)]
+            remote(block, block, ss.at[at, d - 1], rs.at[at, d - 1], head_to(d)).wait_recv()
+        term = buf[at, 0].astype(F32)
+        for h in range(1, heads):
+            term = term + buf[at, h].astype(F32)
+        return term
+
+    over(chunks, own_root)
+    for at, term in enumerate((branch_value_term, branch_key_term)):
+        to_heads(branch_all, at, sweep(term, branch_rows), br_ss, br_rs)
 
     def share_rows(buf, into, ss, rs):
         for d in range(1, n):
@@ -289,24 +305,36 @@
     over(chunks, shares)
     share_rows(att_send, att_recv, at_ss, at_rs)
 
-    def forward(at):
-        for d in range(1, branches):
-            block = root_all.at[at, branch_from(d), my_head]
-            remote(block, block, x_ss.at[at, d - 1], x_rs.at[at, d - 1], branch_to(d)).wait_recv()
-            for e in range(1, heads):
-                send(block, block, hd_ss.at[at, d, e - 1], hd_rs.at[at, d, e - 1], head_to(e))
-
-    for at, out in ((0, bv_out), (1, bk_out)):
-        for d in range(1, heads):
-            block = branch_all.at[at, head_from(d)]
-            remote(block, block, br_ss.at[at, d - 1], br_rs.at[at, d - 1], head_to(d)).wait_recv()
-        term = branch_all[at, 0].astype(F32)
-        for h in range(1, heads):
-            term = term + branch_all[at, h].astype(F32)
-        out[0] = term
-
-    forward(0)
-    forward(1)
+    for e in range(1, branches):
+        for far, ss, rs in ((q_far, xq_ss, xq_rs), (g_far, xg_ss, xg_rs)):
+            for d in range(n):
+                rows = far.at[e - 1, pl.ds(pl.multiple_of(seq_from(d) * own, 16), own)]
+                remote(rows, rows, ss.at[e - 1, d], rs.at[e - 1, d], branch_to(e)).wait_recv()
+        norms = place_far.at[e - 1]
+        remote(norms, norms, x_ss.at[e - 1], x_rs.at[e - 1], branch_to(e)).wait_recv()
+
+    def far_score(e, c):
+        return dot_last(keys[:root_rows, :], q_far[e - 1, rows_of(c), :]) * scale
+
+    def far_values(e, c):
+        term = root_value_term(far_score(e, c), place_far[e - 1, c], g_far[e - 1, rows_of(c), :])
+        put(0, branch_from(e), c, term)
+
+    def far_keys(e, c):
+        gap = dot_last(values[:root_rows, :], g_far[e - 1, rows_of(c), :])
+        q = q_far[e - 1, rows_of(c), :]
+        put(1, branch_from(e), c, root_key_term(far_score(e, c), gap, place_far[e - 1, c], q)[1])
+
+    for at, far in enumerate((far_values, far_keys)):
+        for e in range(1, branches):
+            over(chunks, functools.partial(far, e))
+        term = terms[at, 0]
+        for b in range(1, branches):
+            term = term + terms[at, b]
+        to_heads(root_all, at, term, rs_ss, rs_rs)
+
+    bv_out[0] = from_heads(branch_all, 0, br_ss, br_rs)
+    bk_out[0] = from_heads(branch_all, 1, br_ss, br_rs)
 
     for at, (buf, into, ss, rs, out) in enumerate((
         (dq_send, dq_recv, dq_ss, dq_rs, dq_out), (att_send, att_recv, at_ss, at_rs, att_out)
@@ -321,18 +349,8 @@
         for i in range(answers):
             out[0, i] = rows_f32[at, i * per:(i + 1) * per, :].astype(out.dtype)
 
-    for at, out in ((0, rv_out), (1, rk_out)):
-        for b in range(branches):
-            for d in range(1, heads):
-                block = root_all.at[at, lax.rem(my_branch - b + branches, branches), head_from(d)]
-                remote(
-                    block, block, hd_ss.at[at, b, d - 1], hd_rs.at[at, b, d - 1], head_to(d)
-                ).wait_recv()
-        for h in range(heads):
-            term = root_all[at, 0, h].astype(F32)
-            for b in range(1, branches):
-                term = term + root_all[at, b, h].astype(F32)
-            out[h * piece:(h + 1) * piece, :] = term
+    rv_out[...] = from_heads(root_all, 0, rs_ss, rs_rs)
+    rk_out[...] = from_heads(root_all, 1, rs_ss, rs_rs)
 
     for copy in sends:
         copy.wait_send()
@@ -356,7 +374,6 @@
     chunks = padded // ROWS
     root_rows, branch_rows = root_keys.shape[0], branch_keys.shape[1]
     key_rows = root_rows + branch_rows
-    piece = root_rows // heads
     vmem = pl.BlockSpec(memory_space=pltpu.VMEM)
     whole = pl.BlockSpec(memory_space=pltpu.HBM)
 
@@ -380,19 +397,20 @@
         pltpu.VMEM((chunks, 8, ROWS), F32),
         pltpu.VMEM((padded, width), BF16),
         pltpu.VMEM((z, own, width), BF16),
-        pltpu.VMEM((2, piece, width), F32),
         pltpu.VMEM((padded, width), BF16),
         pltpu.VMEM((z, own, width), BF16),
-        pltpu.VMEM((2, h, piece, width), BF16),
-        pltpu.VMEM((2, h, piece, width), BF16),
-        pltpu.VMEM((2, branches, heads, piece, width), BF16),
+        pltpu.VMEM((b, padded, width), BF16),
+        pltpu.VMEM((b, padded, width), BF16),
+        pltpu.VMEM((b, chunks, 8, ROWS), F32),
+        pltpu.VMEM((2, branches, root_rows, width), F32),
+        pltpu.VMEM((2, heads, root_rows, width), BF16),
         pltpu.VMEM((2, heads, branch_rows, width), BF16),
         pltpu.VMEM((chunks, key_rows, ROWS), BF16),
-        pltpu.VMEM((max(root_rows, branch_rows), width), F32),
+        pltpu.VMEM((branch_rows, width), F32),
         sem(7),
         sem(z), sem(z), sem(z), sem(z), sem(z), sem(z), sem(z), sem(z), sem(z), sem(z),
-        sem(2, h), sem(2, h), sem(2, b), sem(2, b),
-        sem(2, branches, h), sem(2, branches, h), sem(2, h), sem(2, h),
+        sem(2, h), sem(2, h), sem(b), sem(b),
+        sem(b, n), sem(b, n), sem(b, n), sem(b, n), sem(2, h), sem(2, h),
     ]
     outs = (
         jax.ShapeDtypeStruct(queries.shape, BF16),

time: 22.7 us -> 20.9 us (0.921)
  Pallas kernels: 21.9 us -> 20.1 us
    pallas_call x1, Pallas kernels: 20.9 us -> 19.1 us  [per_device(): pl.pallas_call(functools.partial(kernel, sizes), out_shape=outs, in_specs...]
where the time goes in v6:
time: 20.9 us; the launch traced here: 20.8 us
  Pallas kernels  20.1 us (96%)
  between operations  0.64 us (3%)
    pallas_call x1, Pallas kernels, per_device(): pl.pallas_call(functools.partial(kernel, sizes), out_shape=outs, in_specs...  19.1 us
    pallas_call x1, Pallas kernels, per_device(): pl.pallas_call(hand_out, out_shape=outs, in_specs=[vmem] * 6, out_specs=[...  1.03 us

profile of v6, /device:TPU:0, one launch (start us, length us, event | category | flops | bytes accessed | tf_op | source)
XLA Modules:
  0.0 20.8 jit_solution(9034181331893563362)
XLA Ops:
  0.6 19.1 %shard_map.118 = (bf16[1,12,4,128]{3,2,1,0:T(4,128)(2,1)S(1)}, f32[1,12,4,128]{3,2,1,0:T(4,128)S(1)}, f32[512,128]{1,0:T(8,128)S(1)}, f32[512,128]{1,0:T(8,128)S...) custom-call(bf16[48,128]{1,0:T(8,128)(2,1)} %bitcast.2, bf16[48,128]{1,0:T(8,128)(2,1)} %bitcast.3, ...), custom_call_target="tpu_custom_call" | custom-call | tf_op jit(solution)/shard_map/pallas_call | solution.py:423
  19.7 1.0 %shard_map.119 = (bf16[1,12,4,128]{3,2,1,0:T(4,128)(2,1)}, f32[1,12,4,128]{3,2,1,0:T(4,128)}, f32[512,128]{1,0:T(8,128)}, f32[512,128]{1,0:T(8,128)}, f32[1,512,128]{2,1,0:T(8,128)}, /*index=5*/f32[1,512,128]{2,1,0:T(8,128)}) custom-call(bf16[1,12,4,128]{3,2,1,0:T(4,128)(2,1)S(1)} %get-tuple-element.12.refs_0_, ...), custom_call_target="tpu_custom_call" | custom-call | tf_op jit(solution)/shard_map/pallas_call | solution.py:439

commit v7 on v6

--- a/solution.py
+++ b/solution.py
@@ -46,7 +46,7 @@
     att_out, dq_out, rk_out, rv_out, bk_out, bv_out,
     pos_ref, keys, values, keys_t, values_t, rows_f32, qbuf, gbuf, stats, probs, product, weighted, place,
     att_send, att_recv, dq_send, dq_recv,
-    q_far, g_far, place_far, terms, root_all, branch_all, slope, grads,
+    q_far, g_far, score_far, place_far, terms, root_all, branch_all, slope, grads,
     load_sem, q_ss, q_rs, g_ss, g_rs, st_ss, st_rs, at_ss, at_rs, dq_ss, dq_rs,
     rs_ss, rs_rs, x_ss, x_rs, xq_ss, xq_rs, xg_ss, xg_rs, br_ss, br_rs,
 ):
@@ -108,18 +108,18 @@
         copy.start()
         sends.append(copy)
 
-    for load, buf, ss, rs in ((loads[0], qbuf, q_ss, q_rs), (loads[1], gbuf, g_ss, g_rs)):
-        load.wait()
+    for source, buf, ss, rs in ((q_hbm, qbuf, q_ss, q_rs), (g_hbm, gbuf, g_ss, g_rs)):
         for d in range(1, n):
-            send(buf.at[mine], buf.at[mine], ss.at[d - 1], rs.at[d - 1], seq_to(d))
+            send(source, buf.at[mine], ss.at[d - 1], rs.at[d - 1], seq_to(d))
 
     def across(buf, far, ss, rs, d):
         rows = pl.ds(pl.multiple_of(seq_from(d) * own, 16), own)
+        source = buf if d == 0 else buf.at[rows]
         for e in range(1, branches):
-            send(buf.at[rows], far.at[e - 1, rows], ss.at[e - 1, d], rs.at[e - 1, d], branch_to(e))
-
-    across(qbuf, q_far, xq_ss, xq_rs, 0)
-    across(gbuf, g_far, xg_ss, xg_rs, 0)
+            send(source, far.at[e - 1, rows], ss.at[e - 1, d], rs.at[e - 1, d], branch_to(e))
+
+    across(q_hbm, q_far, xq_ss, xq_rs, 0)
+    across(g_hbm, g_far, xg_ss, xg_rs, 0)
 
     if padded > n * own:
         for target in (qbuf, gbuf):
@@ -149,7 +149,7 @@
 
     over(chunks, expand)
 
-    for load in loads[3:]:
+    for load in loads[:2] + loads[3:]:
         load.wait()
     values_t[...] = values[...].astype(F32).T.astype(BF16)
     arrived_rows(qbuf, q_ss, q_rs, q_far, xq_ss, xq_rs)
@@ -174,9 +174,8 @@
         probs[c, :root_rows, :] = on_root
         probs[c, root_rows:, :] = p_branch
         sums = jnp.sum(p_root, axis=0, keepdims=True) + jnp.sum(p_branch, axis=0, keepdims=True)
-        share = dot_plain(values_t[:, :root_rows], p_root.astype(BF16))
-        share = share + dot_plain(values_t[:, root_rows:], p_branch.astype(BF16))
-        weighted[c] = share
+        slope[c, :root_rows, :] = p_root.astype(BF16)
+        slope[c, root_rows:, :] = p_branch.astype(BF16)
         stats[me, c, 0:1, :] = peak
         stats[me, c, 1:2, :] = sums
 
@@ -185,7 +184,9 @@
 
     def dots(c):
         turned = gbuf[rows_of(c), :].astype(F32).T
-        stats[me, c, 2:3, :] = jnp.sum(weighted[c] * turned, axis=0, keepdims=True)
+        share = dot_plain(values_t[...], slope[c])
+        weighted[c] = share
+        stats[me, c, 2:3, :] = jnp.sum(share * turned, axis=0, keepdims=True)
         stats[me, c, 3:8, :] = jnp.zeros((5, ROWS), F32)
 
     over(chunks, dots)
@@ -199,6 +200,22 @@
 
     over(chunks, products)
     keys_t[...] = keys[...].astype(F32).T.astype(BF16)
+
+    def arrived_far(far, ss, rs):
+        for e in range(1, branches):
+            for d in range(n):
+                rows = far.at[e - 1, pl.ds(pl.multiple_of(seq_from(d) * own, 16), own)]
+                remote(rows, rows, ss.at[e - 1, d], rs.at[e - 1, d], branch_to(e)).wait_recv()
+
+    arrived_far(q_far, xq_ss, xq_rs)
+    for e in range(1, branches):
+
+        def far_scores(c, e=e):
+            q = q_far[e - 1, rows_of(c), :]
+            score_far[e - 1, c] = dot_last(keys[:root_rows, :], q) * scale
+
+        over(chunks, far_scores)
+
     for d in range(1, n):
         at = seq_from(d)
         remote(stats.at[at], stats.at[at], st_ss.at[d - 1], st_rs.at[d - 1], seq_to(d)).wait_recv()
@@ -305,25 +322,19 @@
     over(chunks, shares)
     share_rows(att_send, att_recv, at_ss, at_rs)
 
+    arrived_far(g_far, xg_ss, xg_rs)
     for e in range(1, branches):
-        for far, ss, rs in ((q_far, xq_ss, xq_rs), (g_far, xg_ss, xg_rs)):
-            for d in range(n):
-                rows = far.at[e - 1, pl.ds(pl.multiple_of(seq_from(d) * own, 16), own)]
-                remote(rows, rows, ss.at[e - 1, d], rs.at[e - 1, d], branch_to(e)).wait_recv()
         norms = place_far.at[e - 1]
         remote(norms, norms, x_ss.at[e - 1], x_rs.at[e - 1], branch_to(e)).wait_recv()
 
-    def far_score(e, c):
-        return dot_last(keys[:root_rows, :], q_far[e - 1, rows_of(c), :]) * scale
-
     def far_values(e, c):
-        term = root_value_term(far_score(e, c), place_far[e - 1, c], g_far[e - 1, rows_of(c), :])
+        term = root_value_term(score_far[e - 1, c], place_far[e - 1, c], g_far[e - 1, rows_of(c), :])
         put(0, branch_from(e), c, term)
 
     def far_keys(e, c):
         gap = dot_last(values[:root_rows, :], g_far[e - 1, rows_of(c), :])
         q = q_far[e - 1, rows_of(c), :]
-        put(1, branch_from(e), c, root_key_term(far_score(e, c), gap, place_far[e - 1, c], q)[1])
+        put(1, branch_from(e), c, root_key_term(score_far[e - 1, c], gap, place_far[e - 1, c], q)[1])
 
     for at, far in enumerate((far_values, far_keys)):
         for e in range(1, branches):
@@ -401,6 +412,7 @@
         pltpu.VMEM((z, own, width), BF16),
         pltpu.VMEM((b, padded, width), BF16),
         pltpu.VMEM((b, padded, width), BF16),
+        pltpu.VMEM((b, chunks, root_rows, ROWS), F32),
         pltpu.VMEM((b, chunks, 8, ROWS), F32),
         pltpu.VMEM((2, branches, root_rows, width), F32),
         pltpu.VMEM((2, heads, root_rows, width), BF16),

time: 20.9 us -> 20.9 us (level)
  no operation moved by 1% of the time
where the time goes in v7:
time: 20.9 us; the launch traced here: 20.7 us
  Pallas kernels  20.1 us (96%)
  between operations  0.64 us (3%)
    pallas_call x1, Pallas kernels, per_device(): pl.pallas_call(functools.partial(kernel, sizes), out_shape=outs, in_specs...  19 us
    pallas_call x1, Pallas kernels, per_device(): pl.pallas_call(hand_out, out_shape=outs, in_specs=[vmem] * 6, out_specs=[...  1.03 us

profile of v7, /device:TPU:0, one launch (start us, length us, event | category | flops | bytes accessed | tf_op | source)
XLA Modules:
  0.0 20.7 jit_solution(3455963612934483742)
XLA Ops:
  0.6 19.0 %shard_map.118 = (bf16[1,12,4,128]{3,2,1,0:T(4,128)(2,1)S(1)}, f32[1,12,4,128]{3,2,1,0:T(4,128)S(1)}, f32[512,128]{1,0:T(8,128)S(1)}, f32[512,128]{1,0:T(8,128)S...) custom-call(bf16[48,128]{1,0:T(8,128)(2,1)} %bitcast.2, bf16[48,128]{1,0:T(8,128)(2,1)} %bitcast.3, ...), custom_call_target="tpu_custom_call" | custom-call | tf_op jit(solution)/shard_map/pallas_call | solution.py:435
  19.7 1.0 %shard_map.119 = (bf16[1,12,4,128]{3,2,1,0:T(4,128)(2,1)}, f32[1,12,4,128]{3,2,1,0:T(4,128)}, f32[512,128]{1,0:T(8,128)}, f32[512,128]{1,0:T(8,128)}, f32[1,512,128]{2,1,0:T(8,128)}, /*index=5*/f32[1,512,128]{2,1,0:T(8,128)}) custom-call(bf16[1,12,4,128]{3,2,1,0:T(4,128)(2,1)S(1)} %get-tuple-element.12.refs_0_, ...), custom_call_target="tpu_custom_call" | custom-call | tf_op jit(solution)/shard_map/pallas_call | solution.py:451

commit v8 on v7

--- a/solution.py
+++ b/solution.py
@@ -161,6 +161,18 @@
     def rows_of(c):
         return pl.ds(c * ROWS if isinstance(c, int) else pl.multiple_of(c * ROWS, ROWS), ROWS)
 
+    half = ROWS // 2
+
+    def note(c, kind, row):
+        stats[me, c, 2 * kind:2 * kind + 1, :] = row[:, :half]
+        stats[me, c, 2 * kind + 1:2 * kind + 2, :] = row[:, half:]
+
+    def noted(s, c, kind):
+        first, last = 2 * kind, 2 * kind + 1
+        return jnp.concatenate(
+            [stats[s, c, first:first + 1, :], stats[s, c, last:last + 1, :]], axis=1
+        )
+
     def scores(c):
         q = qbuf[rows_of(c), :]
         on_root = dot_last(keys[:root_rows, :], q) * scale
@@ -176,8 +188,8 @@
         sums = jnp.sum(p_root, axis=0, keepdims=True) + jnp.sum(p_branch, axis=0, keepdims=True)
         slope[c, :root_rows, :] = p_root.astype(BF16)
         slope[c, root_rows:, :] = p_branch.astype(BF16)
-        stats[me, c, 0:1, :] = peak
-        stats[me, c, 1:2, :] = sums
+        note(c, 0, peak)
+        note(c, 1, sums)
 
     over(chunks, scores)
     arrived_rows(gbuf, g_ss, g_rs, g_far, xg_ss, xg_rs)
@@ -186,8 +198,8 @@
         turned = gbuf[rows_of(c), :].astype(F32).T
         share = dot_plain(values_t[...], slope[c])
         weighted[c] = share
-        stats[me, c, 2:3, :] = jnp.sum(share * turned, axis=0, keepdims=True)
-        stats[me, c, 3:8, :] = jnp.zeros((5, ROWS), F32)
+        note(c, 2, jnp.sum(share * turned, axis=0, keepdims=True))
+        stats[me, c, 6:8, :] = jnp.zeros((2, half), F32)
 
     over(chunks, dots)
     for d in range(1, n):
@@ -221,15 +233,15 @@
         remote(stats.at[at], stats.at[at], st_ss.at[d - 1], st_rs.at[d - 1], seq_to(d)).wait_recv()
 
     def combine(c):
-        peak = stats[0, c, 0:1, :]
+        peak = noted(0, c, 0)
         for s in range(1, n):
-            peak = jnp.maximum(peak, stats[s, c, 0:1, :])
+            peak = jnp.maximum(peak, noted(s, c, 0))
         sums, dotted = jnp.zeros((1, ROWS), F32), jnp.zeros((1, ROWS), F32)
         for s in range(n):
-            factor = jnp.exp(stats[s, c, 0:1, :] - peak)
-            sums = sums + stats[s, c, 1:2, :] * factor
-            dotted = dotted + stats[s, c, 2:3, :] * factor
-        factor = jnp.exp(stats[me, c, 0:1, :] - peak) / sums
+            factor = jnp.exp(noted(s, c, 0) - peak)
+            sums = sums + noted(s, c, 1) * factor
+            dotted = dotted + noted(s, c, 2) * factor
+        factor = jnp.exp(noted(me, c, 0) - peak) / sums
         place[c, 1:2, :] = factor
         place[c, 2:3, :] = dotted / sums
         place[c, 3:4, :] = peak
@@ -239,6 +251,17 @@
 
     for e in range(1, branches):
         send(place, place_far.at[e - 1], x_ss.at[e - 1], x_rs.at[e - 1], branch_to(e))
+
+    def share_rows(buf, into, ss, rs):
+        for d in range(1, n):
+            far = pl.ds(pl.multiple_of(lax.rem(me + d, n) * own, 16), own)
+            send(buf.at[far], into.at[d - 1], ss.at[d - 1], rs.at[d - 1], seq_to(d))
+
+    def shares(c):
+        att_send[rows_of(c), :] = (weighted[c] * place[c, 1:2, :]).T.astype(BF16)
+
+    over(chunks, shares)
+    share_rows(att_send, att_recv, at_ss, at_rs)
 
     def root_weights(score, norm):
         return jnp.exp(score - norm[3:4, :]) * norm[4:5, :]
@@ -257,12 +280,15 @@
         kept = jnp.where(c == 0, 0.0, terms[at, branch])
         terms[at, branch] = kept + term
 
-    def own_root(c):
+    def own_root_keys(c):
+        score, gap = probs[c, :root_rows, :], product[c, :root_rows, :]
+        sloped, term = root_key_term(score, gap, place[c], qbuf[rows_of(c), :])
+        slope[c, :root_rows, :] = sloped
+        put(1, my_branch, c, term)
+
+    def own_root_values(c):
         score, norm = probs[c, :root_rows, :], place[c]
         put(0, my_branch, c, root_value_term(score, norm, gbuf[rows_of(c), :]))
-        sloped, term = root_key_term(score, product[c, :root_rows, :], norm, qbuf[rows_of(c), :])
-        slope[c, :root_rows, :] = sloped
-        put(1, my_branch, c, term)
 
     def branch_value_term(c):
         weights = probs[c, root_rows:, :] * place[c, 1:2, :]
@@ -301,26 +327,16 @@
             term = term + buf[at, h].astype(F32)
         return term
 
-    over(chunks, own_root)
-    for at, term in enumerate((branch_value_term, branch_key_term)):
-        to_heads(branch_all, at, sweep(term, branch_rows), br_ss, br_rs)
-
-    def share_rows(buf, into, ss, rs):
-        for d in range(1, n):
-            far = pl.ds(pl.multiple_of(lax.rem(me + d, n) * own, 16), own)
-            send(buf.at[far], into.at[d - 1], ss.at[d - 1], rs.at[d - 1], seq_to(d))
-
     def query_terms(c):
         term = dot_plain(keys_t[...], slope[c]) * scale
         dq_send[rows_of(c), :] = term.T.astype(BF16)
 
-    def shares(c):
-        att_send[rows_of(c), :] = (weighted[c] * place[c, 1:2, :]).T.astype(BF16)
-
+    over(chunks, own_root_keys)
+    to_heads(branch_all, 1, sweep(branch_key_term, branch_rows), br_ss, br_rs)
     over(chunks, query_terms)
     share_rows(dq_send, dq_recv, dq_ss, dq_rs)
-    over(chunks, shares)
-    share_rows(att_send, att_recv, at_ss, at_rs)
+    to_heads(branch_all, 0, sweep(branch_value_term, branch_rows), br_ss, br_rs)
+    over(chunks, own_root_values)
 
     arrived_far(g_far, xg_ss, xg_rs)
     for e in range(1, branches):
@@ -401,7 +417,7 @@
         pltpu.VMEM((2, own, width), F32),
         pltpu.VMEM((padded, width), BF16),
         pltpu.VMEM((padded, width), BF16),
-        pltpu.VMEM((n, chunks, 8, ROWS), F32),
+        pltpu.VMEM((n, chunks, 8, ROWS // 2), F32),
         pltpu.VMEM((chunks, key_rows, ROWS), F32),
         pltpu.VMEM((chunks, key_rows, ROWS), F32),
         pltpu.VMEM((chunks, width, ROWS), F32),

time: 20.9 us -> 20.9 us (level)
  no operation moved by 1% of the time
where the time goes in v8:
time: 20.9 us; the launch traced here: 20.8 us
  Pallas kernels  20.1 us (96%)
  between operations  0.64 us (3%)
    pallas_call x1, Pallas kernels, per_device(): pl.pallas_call(functools.partial(kernel, sizes), out_shape=outs, in_specs...  19.1 us
    pallas_call x1, Pallas kernels, per_device(): pl.pallas_call(hand_out, out_shape=outs, in_specs=[vmem] * 6, out_specs=[...  1.03 us

profile of v8, /device:TPU:0, one launch (start us, length us, event | category | flops | bytes accessed | tf_op | source)
XLA Modules:
  0.0 20.8 jit_solution(12219520406102402550)
XLA Ops:
  0.6 19.1 %shard_map.118 = (bf16[1,12,4,128]{3,2,1,0:T(4,128)(2,1)S(1)}, f32[1,12,4,128]{3,2,1,0:T(4,128)S(1)}, f32[512,128]{1,0:T(8,128)S(1)}, f32[512,128]{1,0:T(8,128)S...) custom-call(bf16[48,128]{1,0:T(8,128)(2,1)} %bitcast.2, bf16[48,128]{1,0:T(8,128)(2,1)} %bitcast.3, ...), custom_call_target="tpu_custom_call" | custom-call | tf_op jit(solution)/shard_map/pallas_call | solution.py:451
  19.7 1.0 %shard_map.119 = (bf16[1,12,4,128]{3,2,1,0:T(4,128)(2,1)}, f32[1,12,4,128]{3,2,1,0:T(4,128)}, f32[512,128]{1,0:T(8,128)}, f32[512,128]{1,0:T(8,128)}, f32[1,512,128]{2,1,0:T(8,128)}, /*index=5*/f32[1,512,128]{2,1,0:T(8,128)}) custom-call(bf16[1,12,4,128]{3,2,1,0:T(4,128)(2,1)S(1)} %get-tuple-element.12.refs_0_, ...), custom_call_target="tpu_custom_call" | custom-call | tf_op jit(solution)/shard_map/pallas_call | solution.py:467
